TPU v7x, 32 devices: a whole 2x2x4 slice. The times are simulated.
32 devices in a mesh: member: 4 (over z), token: 8 (over y, x, core).
Axes of the slice: x: 2, y: 2, z: 4, core: 2. Of those that a mesh axis runs over, the one named last changes fastest.
Arguments:
- members_in: bfloat16 [8, 1024, 1024], P('member', 'token'), may hold values from -6 to 6
- member_noise: bfloat16 [8, 1024, 1024], P('member', 'token'), may hold values from -6 to 6
- norm_gain: float32 [1024], replicated, may hold values from 0.25 to 1.75
- weight_query: bfloat16 [1024, 1024], replicated, may hold values from -0.1875 to 0.1875
- weight_key: bfloat16 [1024, 1024], replicated, may hold values from -0.1875 to 0.1875
- weight_value: bfloat16 [1024, 1024], replicated, may hold values from -0.1875 to 0.1875
- weight_out: bfloat16 [1024, 1024], replicated, may hold values from -0.1875 to 0.1875
- decoder_projection_weight: bfloat16 [100, 1024], replicated, may hold values from -0.1875 to 0.1875
- decoder_bias: float32 [100], replicated, may hold values from -3 to 3
- observations: float32 [100, 8192], P(None, 'token'), may hold values from -6 to 6
- surface_extent_factor: float32 [8192], P('token'), may hold values from 0.3 to 3
- quantity_scoring_factor: float32 [100], replicated, may hold values from 0.2 to 2
- point_map: int32 [8192], P('token'), may hold values from 0 to 127
Outputs:
- mean_scoring: float32 [], replicated
- grad_members: bfloat16 [8, 1024, 1024], P('member', 'token')
- grad_out: float32 [1024, 1024], P('token')
- grad_decoder: float32 [100, 1024], replicated
Inputs may be any that keep to these rules, and one draw needn't show every extreme that they name: Point p belongs to token (p // 1024) * 128 + point_map[p].
All inputs are finite; a program needn't handle non-finite values.
Results may differ from a plain program's by a relative error of at most 0.015.
Values may be sent and summed in bfloat16 or wider, within the bound.
A program may use at most 128 MiB of HBM per device.

v0:
```python
import jax
import jax.numpy as jnp
from jax import lax
from jax.sharding import PartitionSpec as P

HEADS = 16
HALF = 128


EPSILON = 1e-06
SMOOTH = 0.01


def extended_2(block, sides, width):
    for axis, dim in sides:
        count = lax.axis_size(axis)
        forward = [(i, i + 1) for i in range(count - 1)]
        backward = [(target, source) for source, target in forward]
        low = lax.ppermute(
            lax.slice_in_dim(block, block.shape[dim] - width, None, axis=dim), axis, forward
        )
        high = lax.ppermute(lax.slice_in_dim(block, 0, width, axis=dim), axis, backward)
        block = jnp.concatenate([low, block, high], axis=dim)
    return block


def from_behind(block, axis, distance):
    devices = range(lax.axis_size(axis))
    route = [(i - distance, i) for i in devices if i - distance in devices]
    return lax.ppermute(block, axis, route)


def normalize_heads(flat):
    rows, width = flat.shape
    split = flat.reshape(rows, HEADS, width // HEADS)
    split = split * lax.rsqrt(jnp.mean(split * split, axis=-1, keepdims=True) + EPSILON)
    return split.reshape(rows, width)


def project(state_in, member_noise, norm_gain, weight_query, weight_key, weight_value):
    member_rows, tokens, width = state_in.shape
    mixed = state_in + member_noise.astype(jnp.float32)
    normed = (
        mixed * lax.rsqrt(jnp.mean(mixed * mixed, axis=-1, keepdims=True) + EPSILON) * norm_gain
    ).astype(jnp.bfloat16)
    flat = normed.reshape(member_rows * tokens, width)
    query = normalize_heads(jnp.dot(flat, weight_query, preferred_element_type=jnp.float32)).astype(
        jnp.bfloat16
    )
    key = normalize_heads(jnp.dot(flat, weight_key, preferred_element_type=jnp.float32)).astype(
        jnp.bfloat16
    )
    value = jnp.dot(flat, weight_value, preferred_element_type=jnp.float32).astype(jnp.bfloat16)
    full_shape = (member_rows, tokens, width)
    return (query.reshape(full_shape), key.reshape(full_shape), value.reshape(full_shape))


def attend(query, keys, values, leading_realization, total):
    member_rows, queries, width = query.shape
    realization_number = keys.shape[1]
    depth = width // HEADS
    query_heads = query.reshape(member_rows, queries, HEADS, depth)
    key_heads = keys.reshape(member_rows, realization_number, HEADS, depth)
    value_heads = values.reshape(member_rows, realization_number, HEADS, depth)
    scores = jnp.einsum(
        "mqhd,mkhd->mhqk", query_heads, key_heads, preferred_element_type=jnp.float32
    ) / jnp.sqrt(jnp.float32(depth))
    query_pos = leading_realization + lax.iota(jnp.int32, queries)
    key_pos = leading_realization - HALF + lax.iota(jnp.int32, realization_number)
    allowed = (key_pos[None, :] >= query_pos[:, None] - HALF) & (
        key_pos[None, :] < query_pos[:, None] + HALF
    )
    allowed = allowed & (key_pos[None, :] >= 0) & (key_pos[None, :] < total)
    raised = jnp.where(allowed[None, None], jnp.exp(scores), jnp.float32(0.0))
    probs = (raised / jnp.sum(raised, axis=-1, keepdims=True)).astype(jnp.bfloat16)
    mixed = jnp.einsum("mhqk,mkhd->mqhd", probs, value_heads, preferred_element_type=jnp.float32)
    return mixed.reshape(member_rows, queries, width).astype(jnp.bfloat16)


def softened_magnitude(diff):
    return jnp.sqrt(diff * diff + SMOOTH)


def unbiased_ranked_score(
    realization_prediction, observed_grid, surface_extent, quantity_scoring_factor
):
    realization_number = realization_prediction.shape[0]
    accuracy_part = softened_magnitude(realization_prediction[0] - observed_grid)
    for realization_position in range(1, realization_number):
        accuracy_part = accuracy_part + softened_magnitude(
            realization_prediction[realization_position] - observed_grid
        )
    dispersion_part = jnp.zeros_like(accuracy_part)
    for leading_realization in range(realization_number):
        for paired_realization in range(leading_realization + 1, realization_number):
            dispersion_part = dispersion_part + softened_magnitude(
                realization_prediction[leading_realization]
                - realization_prediction[paired_realization]
            )
    score = accuracy_part / realization_number - dispersion_part / (
        realization_number * (realization_number - 1)
    )
    return jnp.sum(quantity_scoring_factor[:, None] * surface_extent[None, :] * score)


def shards(
    members_in,
    member_noise,
    norm_gain,
    weight_query,
    weight_key,
    weight_value,
    weight_out,
    decoder_projection_weight,
    decoder_bias,
    observations,
    surface_extent_factor,
    quantity_scoring_factor,
    point_map,
):
    member_rows, tokens, width = members_in.shape
    state = members_in.astype(jnp.float32)

    def front(state_in):
        return project(state_in, member_noise, norm_gain, weight_query, weight_key, weight_value)

    (query, key, value), front_pull = jax.vjp(front, state)
    stacked = jnp.stack([key, value])
    extended = extended_2(stacked, (("token", 2),), HALF)
    leading_realization = lax.axis_index("token") * tokens
    total = tokens * lax.axis_size("token")

    def middle(query_in, extended_in):
        return attend(query_in, extended_in[0], extended_in[1], leading_realization, total)

    attended, middle_pull = jax.vjp(middle, query, extended)
    flat_att = attended.reshape(member_rows * tokens, width)
    update = jnp.dot(flat_att, weight_out, preferred_element_type=jnp.float32).reshape(
        member_rows, tokens, width
    )
    residual_stream_state = (state + member_noise.astype(jnp.float32) + update).astype(jnp.bfloat16)

    def decode_tokens(residual_in, decoder_in):
        mapping_array = jnp.einsum(
            "vc,mtc->mvt",
            decoder_in.astype(jnp.bfloat16),
            residual_in,
            preferred_element_type=jnp.float32,
        )
        mapping_array = mapping_array + decoder_bias[None, :, None]
        return jnp.take(mapping_array, point_map, axis=2)

    realization_prediction, readout_slope_pulled = jax.vjp(
        decode_tokens, residual_stream_state, decoder_projection_weight.astype(jnp.float32)
    )
    location_places = realization_prediction.shape[2]
    groups = lax.axis_size("member")
    local_shard = lax.axis_index("member")
    gathered_lines = lax.all_gather(realization_prediction, "member", axis=0, tiled=True)

    def score_all(whole):
        return unbiased_ranked_score(
            whole, observations, surface_extent_factor, quantity_scoring_factor
        )

    full_loss, score_pull = jax.vjp(score_all, gathered_lines)
    (complete_gradient,) = score_pull(jnp.ones((), jnp.float32))
    prediction_slope = lax.dynamic_slice_in_dim(
        complete_gradient, local_shard * member_rows, member_rows, 0
    )
    partial_loss = full_loss / groups
    carried_slope, readout_piece_result = readout_slope_pulled(prediction_slope)
    overall_scoring_amount, grad_decoder = lax.psum(
        (partial_loss, readout_piece_result), ("member", "token")
    )
    mean_scoring = overall_scoring_amount / (
        realization_prediction.shape[1] * location_places * lax.axis_size("token")
    )
    flat_grad = carried_slope.reshape(member_rows * tokens, width)
    grad_attended = (
        jnp.dot(flat_grad, weight_out.T, preferred_element_type=jnp.float32)
        .astype(jnp.bfloat16)
        .reshape(member_rows, tokens, width)
    )
    grad_query, grad_extended = middle_pull(grad_attended)
    lower_rim = grad_extended[:, :, :HALF]
    upper_rim = grad_extended[:, :, tokens + HALF :]
    inner = grad_extended[:, :, HALF : tokens + HALF].astype(jnp.float32)
    from_next = from_behind(lower_rim, "token", -1)
    from_prev = from_behind(upper_rim, "token", 1)
    inner = inner.at[:, :, tokens - HALF :].add(from_next.astype(jnp.float32))
    inner = inner.at[:, :, :HALF].add(from_prev.astype(jnp.float32))
    (grad_front,) = front_pull(
        (grad_query, inner[0].astype(jnp.bfloat16), inner[1].astype(jnp.bfloat16))
    )
    grad_members = (grad_front + carried_slope.astype(jnp.float32)).astype(jnp.bfloat16)
    contract = (((0,), (0,)), ((), ()))
    product = lax.dot_general(flat_att, flat_grad, contract, preferred_element_type=jnp.float32)
    summed = lax.psum(product.astype(jnp.bfloat16), "member").astype(jnp.float32)
    grad_out = lax.psum_scatter(summed, "token", scatter_dimension=0, tiled=True)
    return (mean_scoring, grad_members, grad_out, grad_decoder)


def solution(mesh):
    return jax.shard_map(
        shards,
        mesh=mesh,
        in_specs=(
            P("member", "token", None),
            P("member", "token", None),
            P(),
            P(),
            P(),
            P(),
            P(),
            P(),
            P(),
            P(None, "token"),
            P("token"),
            P(),
            P("token"),
        ),
        out_specs=(P(), P("member", "token", None), P("token", None), P()),
        check_vma=False,
    )
```

profile of v0, /device:TPU:0, one launch (start us, length us, event | category | flops | bytes accessed | tf_op | source)
XLA Modules:
  0.0 532.4 jit_solution(3759867318628621100)
XLA Ops:
  8.9 3.9 copy.95
  20.3 3.3 convolution_convert_fusion.8
  25.5 3.8 pad_maximum_fusion.1
  29.3 3.3 collective-permute-start
  34.5 3.9 copy.98
  41.7 5.7 %pad_maximum_fusion = bf16[2,2,384,1024]{2,1,3,0:T(2,128)(2,1)S(1)} fusion(bf16[2,2,128,1024]{2,1,3,0:T(2,128)(2,1)} %collective-permute-done.1, bf16[1,2,128,1024]{2,1,3,0:T(2,128)(2,1)S(1)} %copy-done.15, bf16[1,2,128,1024]{2,1,3,0:T(2,128)(2,1)S(1)} %copy-done.14, bf16[2,2,128,1024]{2,1,3,0:T(2,128)(2,1)} %collective-permute-done), kind=kLoop, calls=%fused_computation.22 | loop fusion | flops 12582912 | bytes 6291456 | tf_op jit(solution)/shard_map/concatenate | solution.py:23
  59.6 7.5 %gather_fusion = f32[1024,2,100]{2,1,0:T(2,128)} fusion(f32[2,100,128]{1,0,2:T(2,128)S(1)} %copy.102, s32[1024]{0:T(1024)S(1)} %get-tuple-element.164), kind=kCustom, calls=%fused_computation | custom fusion | bytes 1642496 | tf_op jit(solution)/shard_map/jvp(jit(_take))/gather | solution.py:151
  67.1 6.1 %select_bitcast_fusion = f32[2,100,1024]{1,0,2:T(2,128)} fusion(f32[1024,2,100]{2,1,0:T(2,128)} %gather_fusion, pred[1024]{0:T(1024)(128)(4,1)S(1)} %compare_and_fusion), kind=kLoop, calls=%fused_computation.68 | loop fusion | flops 204800 | bytes 1639424 | tf_op jit(solution)/shard_map/jvp(jit(_take))/select_n | solution.py:151
  75.7 85.2 %all-gather.2.cloned.1.call-done = f32[8,100,1024]{2,1,0:T(8,128)} async-done(((f32[2,100,1024]{2,1,0:T(8,128)}), f32[8,100,1024]{2,1,0:T(8,128)}) %all-gather.2.cloned.1.call-update) | async-done | bytes 3276816 | tf_op jit(solution)/shard_map/all_gather | solution.py:159
  160.9 3.2 fusion.195
  167.5 6.7 %fusion.57 = (f32[1,100,1024]{2,1,0:T(8,128)S(1)}, f32[1,100,1024]{2,1,0:T(8,128)S(1)}, f32[1,100,1024]{2,1,0:T(8,128)S(1)}, f32[1,100,1024]{2,1,0:T(8,128)S(1)}...) fusion(f32[1024]{0:T(1024)S(1)} %copy-done.33, ...), kind=kLoop, calls=%fused_computation.106 | loop fusion | flops 18534400 | bytes 6967700 | tf_op jit(solution)/shard_map/transpose(jvp())/broadcast_in_dim | solution.py:91
  174.2 3.5 pad_add_fusion
  181.4 63.8 %scatter_fusion = f32[2,100,128]{1,0,2:T(2,128)S(1)} fusion(f32[2,100,128]{1,0,2:T(2,128)S(1)} %broadcast_in_dim.59, s32[1024]{0:T(1024)S(1)} %get-tuple-element.163, f32[1024,2,100]{2,1,0:T(2,128)} %copy.104), kind=kCustom, calls=%fused_computation.1 | custom fusion | flops 204800 | bytes 2461696 | tf_op jit(solution)/shard_map/transpose(jvp(jit(_take)))/scatter-add | solution.py:151
  246.5 3.2 bitcast_convert_fusion
  258.0 5.4 %fusion.5 = (f32[2,16,128]{2,1,0:T(8,128)S(1)}, bf16[2,16,128,384]{3,2,1,0:T(8,128)(2,1)}) fusion(f32[2,16,128,384]{3,2,1,0:T(8,128)} %copy-done.11, f32[2,16,128]{2,1,0:T(8,128)S(1)} %multiply_divide_fusion, pred[128,384]{1,0:T(8,128)(4,1)S(1)} %copy-done.30, bf16[2,384,16,64]{1,3,2,0:T(8,128)(2,1)S(1)} %bitcast.510, bf16[2,16,64,128]{3,0,2,1:T(2,128)(2,1)S(1)} %bitcast.515), kind=kOutput, calls=%fused_computation.9 | convolution fusion | flops 212332544 | bytes 11616256 | tf_op jit(solution)/shard_map/transpose(jvp(mhqk,mkhd->mqhd))/dot_general | solution.py:76
  263.4 71.5 %all-reduce.69.cloned.1.call-done = bf16[1024,1024]{1,0:T(8,128)(2,1)} async-done(((bf16[1024,1024]{1,0:T(8,128)(2,1)}), bf16[1024,1024]{1,0:T(8,128)(2,1)}) %all-reduce.69.cloned.1.call-update) | async-done | bytes 2097168 | tf_op jit(solution)/shard_map/psum | solution.py:199
  334.9 4.1 convert_element_type.189
  340.3 5.1 convolution_convert_fusion.2
  355.0 4.0 collective-permute-start.3
  359.7 7.9 %fusion.17 = f32[2,16,8,8,128]{4,3,2,1,0:T(8,128)} fusion(bf16[2,384,16,64]{1,3,2,0:T(8,128)(2,1)} %bitcast.521, bf16[2,16,128,384]{3,2,1,0:T(8,128)(2,1)} %get-tuple-element.172, f32[2,16,128,384]{3,2,1,0:T(8,128)} %copy-done.11, f32[2,16,128]{2,1,0:T(8,128)S(1)} %neg.212, f32[2,16,128]{2,1,0:T(8,128)S(1)} %copy-done.35, pred[128,384]{1,0:T(8,128)(4,1)S(1)} %copy-done.30), kind=kOutput, calls=%fused_computation.46 | convolution fusion | flops 212860928 | bytes 12140544 | tf_op jit(solution)/shard_map/transpose(jvp(mqhd,mkhd->mhqk))/dot_general | solution.py:65
  367.6 44.7 %psum.21 = f32[]{:T(128)} all-reduce(f32[]{:T(128)S(6)} %div.254), channel_id=1, replica_groups=mesh['member'=4,'token'=8] {'member','token'}, use_global_device_ids=true, to_apply=%region_5.6 | all-reduce | flops 1 | bytes 8 | tf_op jit(solution)/shard_map/psum | solution.py:173
  418.3 3.2 add_convert_fusion
  430.5 36.1 %all-reduce.71.cloned.1.call-done = f32[100,1024]{1,0:T(8,128)} async-done(((f32[100,1024]{1,0:T(8,128)}), f32[100,1024]{1,0:T(8,128)}) %all-reduce.71.cloned.1.call-update) | async-done | bytes 409616 | tf_op jit(solution)/shard_map/psum | solution.py:173
  466.6 56.1 %reduce-scatter.2.cloned.1.call-done = f32[128,1024]{1,0:T(8,128)} async-done(((f32[1024,1024]{1,0:T(8,128)}), f32[128,1024]{1,0:T(8,128)}) %reduce-scatter.2.cloned.1.call-update) | async-done | bytes 524304 | tf_op jit(solution)/shard_map/reduce_scatter | solution.py:200
  (169 shorter events, 73.9 us)
Async XLA Ops:
  7.2 48.9 %copy-start = (bf16[1024,1024]{1,0:T(8,128)(2,1)S(1)}, bf16[1024,1024]{1,0:T(8,128)(2,1)}, u32[]{:S(2)}) copy-start(bf16[1024,1024]{1,0:T(8,128)(2,1)} %param.27) | copy-start | bytes 6291460
  7.2 5.6 %copy-start.8 = (bf16[2,128,1024]{2,1,0:T(8,128)(2,1)S(1)}, bf16[2,128,1024]{2,1,0:T(8,128)(2,1)}, u32[]{:S(2)}) copy-start(bf16[2,128,1024]{2,1,0:T(8,128)(2,1)} %param.21) | copy-start | bytes 1572868
  7.2 5.6 %copy-start.7 = (bf16[2,128,1024]{2,1,0:T(8,128)(2,1)S(1)}, bf16[2,128,1024]{2,1,0:T(8,128)(2,1)}, u32[]{:S(2)}) copy-start(bf16[2,128,1024]{2,1,0:T(8,128)(2,1)} %param.22) | copy-start | bytes 1572868
  7.2 5.6 %copy-start.42 = (f32[1024]{0:T(1024)S(1)}, f32[1024]{0:T(1024)}, u32[]{:S(2)}) copy-start(f32[1024]{0:T(1024)} %param.23) | copy-start | bytes 12292
  7.2 153.7 %all-gather.2.cloned.1.call-start = ((), (), s32[]{:S(2)}) async-start(), calls=%async_computation.1 | async-start | bytes 4259840 | tf_op jit(solution)/shard_map/all_gather | solution.py:159
  25.5 12.9 %copy-start.43 = (s32[1024]{0:T(1024)S(1)}, s32[1024]{0:T(1024)}, u32[]{:S(2)}) copy-start(s32[1024]{0:T(1024)} %param.33) | copy-start | bytes 12292
  29.3 12.0 %collective-permute-start = (bf16[2,2,128,1024]{2,1,3,0:T(2,128)(2,1)}, bf16[2,2,128,1024]{2,1,3,0:T(2,128)(2,1)}, u32[]{:S(2)}, u32[]{:S(2)}) collective-permute-start(bf16[2,2,128,1024]{2,1,3,0:T(2,128)(2,1)} %pad_maximum_fusion.1), channel_id=1, source_target_pairs={{0,1},{1,2},{2,3},{3,4},{4,5},{5,6},{6,7},{8,9},{9,10},{10,11},{11... | collective-permute-start | bytes 3145736 | tf_op jit(solution)/shard_map/ppermute | solution.py:19
  32.7 8.6 %collective-permute-start.1 = (bf16[2,2,128,1024]{2,1,3,0:T(2,128)(2,1)}, bf16[2,2,128,1024]{2,1,3,0:T(2,128)(2,1)}, u32[]{:S(2)}, u32[]{:S(2)}) collective-permute-start(bf16[2,2,128,1024]{2,1,3,0:T(2,128)(2,1)} %pad_maximum_fusion.1), channel_id=1, source_target_pairs={{1,0},{2,1},{3,2},{4,3},{5,4},{6,5},{7,6},{9,8},{10,9},{11,10},{12... | collective-permute-start | bytes 3145736 | tf_op jit(solution)/shard_map/ppermute | solution.py:22
  41.1 8.9 %copy-start.20 = (f32[256,16,64]{0,2,1:T(8,128)}, f32[256,16,64]{0,2,1:T(8,128)S(1)}, u32[]{:S(2)}) copy-start(f32[256,16,64]{0,2,1:T(8,128)S(1)} %get-tuple-element.168) | copy-start | bytes 3145732
  41.1 8.9 %copy-start.40 = (f32[256,16]{0,1:T(8,128)}, f32[256,16]{0,1:T(8,128)S(1)}, u32[]{:S(2)}) copy-start(f32[256,16]{0,1:T(8,128)S(1)} %fusion.187) | copy-start | bytes 49156
  41.3 10.6 %copy-start.29 = (pred[128,384]{1,0:T(8,128)(4,1)}, pred[128,384]{1,0:T(8,128)(4,1)S(1)}, u32[]{:S(2)}) copy-start(pred[128,384]{1,0:T(8,128)(4,1)S(1)} %and_and_fusion) | copy-start | bytes 147460
  50.0 4.5 copy-start.12
  58.6 102.3 %copy-start.33 = (f32[1024]{0:T(1024)S(1)}, f32[1024]{0:T(1024)}, u32[]{:S(2)}) copy-start(f32[1024]{0:T(1024)} %param.31) | copy-start | bytes 12292
  58.6 102.3 %copy-start.44 = (f32[100]{0:T(128)S(1)}, f32[100]{0:T(128)}, u32[]{:S(2)}) copy-start(f32[100]{0:T(128)} %param.32) | copy-start | bytes 1204
  75.5 259.4 %all-reduce.69.cloned.1.call-start = ((), (), s32[]{:S(2)}) async-start(), calls=%async_computation.2 | async-start | bytes 4194304 | tf_op jit(solution)/shard_map/psum | solution.py:199
  245.3 4.4 copy-start.35
  249.7 216.9 %all-reduce.71.cloned.1.call-start = ((), (), s32[]{:S(2)}) async-start(), calls=%async_computation.4 | async-start | bytes 851968 | tf_op jit(solution)/shard_map/psum | solution.py:173
  249.7 8.3 %copy-start.30 = (pred[128,384]{1,0:T(8,128)(4,1)S(1)}, pred[128,384]{1,0:T(8,128)(4,1)}, u32[]{:S(2)}) copy-start(pred[128,384]{1,0:T(8,128)(4,1)} %copy-done.29) | copy-start | bytes 147460
  252.3 5.7 %copy-start.13 = (bf16[1,2,384,1024]{2,3,1,0:T(8,128)(2,1)S(1)}, bf16[1,2,384,1024]{2,3,1,0:T(8,128)(2,1)}, u32[]{:S(2)}) copy-start(bf16[1,2,384,1024]{2,3,1,0:T(8,128)(2,1)} %copy-done.12) | copy-start | bytes 4718596
  257.8 264.9 %reduce-scatter.2.cloned.1.call-start = ((), (), s32[]{:S(2)}) async-start(), calls=%async_computation.3 | async-start | bytes 4718592 | tf_op jit(solution)/shard_map/reduce_scatter | solution.py:200
  353.8 64.5 %collective-permute-start.2 = (bf16[2,2,128,1024]{2,1,3,0:T(2,128)(2,1)}, bf16[2,2,128,1024]{2,1,3,0:T(2,128)(2,1)}, u32[]{:S(2)}, u32[]{:S(2)}) collective-permute-start(bf16[2,2,128,1024]{2,1,3,0:T(2,128)(2,1)} %get-tuple-element.157), channel_id=1, source_target_pairs={{1,0},{2,1},{3,2},{4,3},{5,4},{6,5},{7,6},{9,8},{10,9},{11,10},{12... | collective-permute-start | bytes 3145736 | tf_op jit(solution)/shard_map/ppermute | solution.py:30
  355.0 63.2 %collective-permute-start.3 = (bf16[2,2,128,1024]{2,1,3,0:T(2,128)(2,1)}, bf16[2,2,128,1024]{2,1,3,0:T(2,128)(2,1)}, u32[]{:S(2)}, u32[]{:S(2)}) collective-permute-start(bf16[2,2,128,1024]{2,1,3,0:T(2,128)(2,1)} %get-tuple-element.158), channel_id=1, source_target_pairs={{0,1},{1,2},{2,3},{3,4},{4,5},{5,6},{6,7},{8,9},{9,10},{10,11},{11... | collective-permute-start | bytes 3145736 | tf_op jit(solution)/shard_map/ppermute | solution.py:30
  359.7 55.0 %copy-start.39 = (f32[256,16]{0,1:T(8,128)S(1)}, f32[256,16]{0,1:T(8,128)}, u32[]{:S(2)}) copy-start(f32[256,16]{0,1:T(8,128)} %copy-done.38) | copy-start | bytes 49156
  428.1 96.4 %copy-start.1 = (bf16[1024,1024]{1,0:T(8,128)(2,1)S(1)}, bf16[1024,1024]{1,0:T(8,128)(2,1)}, u32[]{:S(2)}) copy-start(bf16[1024,1024]{1,0:T(8,128)(2,1)} %param.27) | copy-start | bytes 6291460
  (32 other events, 63.5 us)
Sparse Core Ops, SparseCore 0:
  75.6 85.2 all-gather.1
  249.8 85.0 all-reduce.68
  341.7 124.8 all-reduce.70
  470.3 52.2 reduce-scatter.1
where the time goes:
time: 543 us; the launch traced here: 532 us
  waiting for transfers between devices  249 us (46%)
  other arithmetic  119 us (22%)
  local copies, waits for them, and re-layouts  47.8 us (9%)
  blocking collectives  44.7 us (8%)
  matrix products  43.5 us (8%)
  between operations  17.3 us (3%)
  starting transfers between devices  11 us (2%)
    all_gather x1, waiting for transfers between devices, shards(): lax.all_gather(realization_prediction, 'member', axis=0, tiled=True)  85.2 us
    psum x1, waiting for transfers between devices, shards(): lax.psum(product.astype(jnp.bfloat16), 'member').astype(jnp.float32)  71.5 us
    scatter-add x1, other arithmetic, decode_tokens(): return jnp.take(mapping_array, point_map, axis=2)  63.8 us
    reduce_scatter x1, waiting for transfers between devices, shards(): lax.psum_scatter(summed, 'token', scatter_dimension=0, tiled=True)  56.1 us
    psum x1, blocking collectives, shards(): lax.psum((partial_loss, readout_piece_result), ('member', 'token'))  44.7 us
    psum x1, waiting for transfers between devices, shards(): lax.psum((partial_loss, readout_piece_result), ('member', 'token'))  36.1 us
    unnamed x99, local copies, waits for them, and re-layouts  19.3 us
    dot_general x3, matrix products, attend(): jnp.einsum('mqhd,mkhd->mhqk', query_heads, key_heads, preferred_element_t...  14.8 us
  transfers between devices with their start and end apart: 8, of which 4 were waited for; matrix products, arithmetic and copies ran while one was open for 11% of the time, Pallas kernels for 0%

commit v1 on v0

--- a/solution.py
+++ b/solution.py
@@ -77,30 +77,41 @@
     return mixed.reshape(member_rows, queries, width).astype(jnp.bfloat16)
 
 
-def softened_magnitude(diff):
-    return jnp.sqrt(diff * diff + SMOOTH)
-
-
-def unbiased_ranked_score(
-    realization_prediction, observed_grid, surface_extent, quantity_scoring_factor
-):
-    realization_number = realization_prediction.shape[0]
-    accuracy_part = softened_magnitude(realization_prediction[0] - observed_grid)
-    for realization_position in range(1, realization_number):
-        accuracy_part = accuracy_part + softened_magnitude(
-            realization_prediction[realization_position] - observed_grid
-        )
-    dispersion_part = jnp.zeros_like(accuracy_part)
-    for leading_realization in range(realization_number):
-        for paired_realization in range(leading_realization + 1, realization_number):
-            dispersion_part = dispersion_part + softened_magnitude(
-                realization_prediction[leading_realization]
-                - realization_prediction[paired_realization]
-            )
-    score = accuracy_part / realization_number - dispersion_part / (
-        realization_number * (realization_number - 1)
-    )
-    return jnp.sum(quantity_scoring_factor[:, None] * surface_extent[None, :] * score)
+def split_product(left, right, equation):
+    high = left.astype(jnp.bfloat16)
+    low = (left - high.astype(jnp.float32)).astype(jnp.bfloat16)
+    first = jnp.einsum(equation, high, right, preferred_element_type=jnp.float32)
+    return first + jnp.einsum(equation, low, right, preferred_element_type=jnp.float32)
+
+
+def score_and_slope(own, observed, surface_extent, quantity, point_map):
+    member_rows, _, tokens = own.shape
+    onehot = point_map[:, None] == lax.iota(jnp.int32, tokens)[None, :]
+    token_area = jnp.sum(jnp.where(onehot, surface_extent[:, None], 0.0), axis=0)
+    onehot = onehot.astype(jnp.bfloat16)
+    everyone = lax.all_gather(own, "member", axis=0, tiled=True)
+    count = everyone.shape[0]
+    diff = split_product(own, onehot, "mvt,pt->mvp") - observed[None]
+    inverse = lax.rsqrt(diff * diff + SMOOTH)
+    weight = quantity[:, None] * surface_extent[None, :] / count
+    weighted = weight[None] * inverse
+    share = jnp.sum(weighted * (diff * diff + SMOOTH))
+    slope = split_product(weighted * diff, onehot, "mvp,pt->mvt")
+    first = lax.axis_index("member") * member_rows
+    pair_weight = quantity[:, None] * token_area[None, :] / (count * (count - 1))
+    for row in range(member_rows):
+        magnitude = jnp.zeros_like(own[0])
+        pulled = jnp.zeros_like(own[0])
+        for other in range(count):
+            gap = own[row] - everyone[other]
+            square = gap * gap + SMOOTH
+            upside = lax.rsqrt(square)
+            keep = jnp.where(first + row == other, 0.0, 0.5)
+            magnitude = magnitude + keep * square * upside
+            pulled = pulled + gap * upside
+        share = share - jnp.sum(pair_weight * magnitude)
+        slope = slope.at[row].add(-pair_weight * pulled)
+    return share, slope
 
 
 def shards(
@@ -140,41 +151,26 @@
     )
     residual_stream_state = (state + member_noise.astype(jnp.float32) + update).astype(jnp.bfloat16)
 
-    def decode_tokens(residual_in, decoder_in):
-        mapping_array = jnp.einsum(
-            "vc,mtc->mvt",
-            decoder_in.astype(jnp.bfloat16),
-            residual_in,
-            preferred_element_type=jnp.float32,
-        )
-        mapping_array = mapping_array + decoder_bias[None, :, None]
-        return jnp.take(mapping_array, point_map, axis=2)
-
-    realization_prediction, readout_slope_pulled = jax.vjp(
-        decode_tokens, residual_stream_state, decoder_projection_weight.astype(jnp.float32)
-    )
-    location_places = realization_prediction.shape[2]
-    groups = lax.axis_size("member")
-    local_shard = lax.axis_index("member")
-    gathered_lines = lax.all_gather(realization_prediction, "member", axis=0, tiled=True)
-
-    def score_all(whole):
-        return unbiased_ranked_score(
-            whole, observations, surface_extent_factor, quantity_scoring_factor
-        )
-
-    full_loss, score_pull = jax.vjp(score_all, gathered_lines)
-    (complete_gradient,) = score_pull(jnp.ones((), jnp.float32))
-    prediction_slope = lax.dynamic_slice_in_dim(
-        complete_gradient, local_shard * member_rows, member_rows, 0
-    )
-    partial_loss = full_loss / groups
-    carried_slope, readout_piece_result = readout_slope_pulled(prediction_slope)
-    overall_scoring_amount, grad_decoder = lax.psum(
-        (partial_loss, readout_piece_result), ("member", "token")
-    )
+    own = jnp.einsum(
+        "vc,mtc->mvt",
+        decoder_projection_weight,
+        residual_stream_state,
+        preferred_element_type=jnp.float32,
+    )
+    own = own + decoder_bias[None, :, None]
+    share, slope = score_and_slope(
+        own, observations, surface_extent_factor, quantity_scoring_factor, point_map
+    )
+    slope = slope.astype(jnp.bfloat16)
+    decoder_piece = jnp.einsum(
+        "mvt,mtc->vc", slope, residual_stream_state, preferred_element_type=jnp.float32
+    )
+    carried_slope = jnp.einsum(
+        "mvt,vc->mtc", slope, decoder_projection_weight, preferred_element_type=jnp.float32
+    ).astype(jnp.bfloat16)
+    overall_scoring_amount, grad_decoder = lax.psum((share, decoder_piece), ("member", "token"))
     mean_scoring = overall_scoring_amount / (
-        realization_prediction.shape[1] * location_places * lax.axis_size("token")
+        observations.shape[0] * observations.shape[1] * lax.axis_size("token")
     )
     flat_grad = carried_slope.reshape(member_rows * tokens, width)
     grad_attended = (
@@ -196,8 +192,10 @@
     grad_members = (grad_front + carried_slope.astype(jnp.float32)).astype(jnp.bfloat16)
     contract = (((0,), (0,)), ((), ()))
     product = lax.dot_general(flat_att, flat_grad, contract, preferred_element_type=jnp.float32)
-    summed = lax.psum(product.astype(jnp.bfloat16), "member").astype(jnp.float32)
-    grad_out = lax.psum_scatter(summed, "token", scatter_dimension=0, tiled=True)
+    scattered = lax.psum_scatter(
+        product.astype(jnp.bfloat16), "token", scatter_dimension=0, tiled=True
+    )
+    grad_out = lax.psum(scattered.astype(jnp.float32), "member")
     return (mean_scoring, grad_members, grad_out, grad_decoder)
 
 

time: 543 us -> 324 us (0.60); the launches traced: 532 us -> 323 us
  waiting for transfers between devices: 249 us -> 78.6 us
  other arithmetic: 119 us -> 29.5 us
  blocking collectives: 44.7 us -> 102 us
  local copies, waits for them, and re-layouts: 47.8 us -> 26.5 us
  starting transfers between devices: 11 us -> 18.7 us
    all_gather x1 -> x0, waiting for transfers between devices: 85.2 us -> none  [shards(): lax.all_gather(realization_prediction, 'member', axis=0, tiled=True)]
    scatter-add x1 -> x2, other arithmetic: 63.8 us -> 0.21 us  [score_and_slope(): slope = slope.at[row].add(-pair_weight * pulled)]
    reduce_scatter x1, waiting for transfers between devices: 56.1 us -> 0.01 us  [shards(): lax.psum_scatter(product.astype(jnp.bfloat16), 'token', scatter_dimension...]
    psum x1 -> x2, blocking collectives: 44.7 us -> 85.6 us  [the longest x1 55.9 us: shards(): lax.psum((share, decoder_piece), ('member', 'token'))]
    psum x2 -> x1, waiting for transfers between devices: 108 us -> 78.6 us  [shards(): lax.psum((share, decoder_piece), ('member', 'token'))]
    all_gather x0 -> x1, blocking collectives: none -> 16.3 us  [score_and_slope(): everyone = lax.all_gather(own, 'member', axis=0, tiled=True)]
    ppermute x2, starting transfers between devices: 5.3 us -> 13.1 us  [from_behind(): return lax.ppermute(block, axis, route)]
    gather x1 -> x0, local copies, waits for them, and re-layouts: 7.49 us -> none  [decode_tokens(): return jnp.take(mapping_array, point_map, axis=2)]
  transfers between devices with their start and end apart: 8 -> 6, of which waited for: 4 -> 1; matrix products, arithmetic and copies ran while one was open for 11% -> 14% of each run, Pallas kernels for 0% -> 0%
where the time goes in v1:
time: 324 us; the launch traced here: 323 us
  blocking collectives  102 us (31%)
  waiting for transfers between devices  78.6 us (24%)
  matrix products  47.5 us (15%)
  other arithmetic  29.5 us (9%)
  local copies, waits for them, and re-layouts  26.5 us (8%)
  between operations  20 us (6%)
  starting transfers between devices  18.7 us (6%)
    psum x1, waiting for transfers between devices, shards(): lax.psum((share, decoder_piece), ('member', 'token'))  78.6 us
    psum x1, blocking collectives, shards(): lax.psum((share, decoder_piece), ('member', 'token'))  55.9 us
    psum x1, blocking collectives, shards(): grad_out = lax.psum(scattered.astype(jnp.float32), 'member')  29.7 us
    all_gather x1, blocking collectives, score_and_slope(): everyone = lax.all_gather(own, 'member', axis=0, tiled=True)  16.3 us
    dot_general x3, matrix products, attend(): jnp.einsum('mqhd,mkhd->mhqk', query_heads, key_heads, preferred_element_t...  16.2 us
    unnamed x67, local copies, waits for them, and re-layouts  15.6 us
    ppermute x2, starting transfers between devices, from_behind(): return lax.ppermute(block, axis, route)  13.1 us
    dot_general x3, matrix products, attend(): jnp.einsum('mhqk,mkhd->mqhd', probs, value_heads, preferred_element_type=...  9.74 us
  transfers between devices with their start and end apart: 6, of which 1 were waited for; matrix products, arithmetic and copies ran while one was open for 14% of the time, Pallas kernels for 0%

profile of v1, /device:TPU:0, one launch (start us, length us, event | category | flops | bytes accessed | tf_op | source)
XLA Modules:
  0.0 322.7 jit_solution(5095685662917015792)
XLA Ops:
  11.1 2.5 convolution_convert_fusion.8
  14.0 4.0 %copy.43 = bf16[1024,1024]{0,1:T(8,128)(2,1)} copy(bf16[1024,1024]{1,0:T(8,128)(2,1)} %param.29) | data formatting | bytes 4194304 | tf_op args[4]
  18.0 2.3 multiply_reduce_fusion.2
  23.4 2.5 pad_maximum_fusion.1
  27.2 4.0 %collective-permute-start = (bf16[2,2,128,1024]{2,1,3,0:T(2,128)(2,1)}, bf16[2,2,128,1024]{2,1,3,0:T(2,128)(2,1)}, u32[]{:S(2)}, u32[]{:S(2)}) collective-permute-start(bf16[2,2,128,1024]{2,1,3,0:T(2,128)(2,1)} %pad_maximum_fusion.1), channel_id=1, source_target_pairs={{0,1},{1,2},{2,3},{3,4},{4,5},{5,6},{6,7},{8,9},{9,10},{10,11},{11... | collective-permute-start | bytes 3145736 | tf_op jit(solution)/shard_map/ppermute | solution.py:19
  31.7 3.9 %copy.46 = bf16[1024,1024]{0,1:T(8,128)(2,1)} copy(bf16[1024,1024]{1,0:T(8,128)(2,1)} %param.28) | data formatting | bytes 4194304 | tf_op args[3]
  35.7 2.5 multiply_reduce_fusion.1
  38.5 5.7 %pad_maximum_fusion = bf16[2,2,384,1024]{2,1,3,0:T(2,128)(2,1)S(1)} fusion(bf16[2,2,128,1024]{2,1,3,0:T(2,128)(2,1)} %collective-permute-done.1, bf16[1,2,128,1024]{2,1,3,0:T(2,128)(2,1)S(1)} %copy.44, bf16[1,2,128,1024]{2,1,3,0:T(2,128)(2,1)S(1)} %convert_element_type.168, bf16[2,2,128,1024]{2,1,3,0:T(2,128)(2,1)} %collective-permute-done), kind=kLoop, calls=%fused_computation.13 | loop fusion | flops 12582912 | bytes 6291456 | tf_op jit(solution)/shard_map/concatenate | solution.py:23
  44.2 2.2 fusion.78
  54.4 16.3 %all_gather.3 = f32[8,100,128]{2,1,0:T(8,128)S(1)} all-gather(f32[2,100,128]{2,1,0:T(8,128)S(1)} %fusion.21), channel_id=1, replica_groups=mesh['member'=4,'token'=8] {'member'}, dimensions={0}, use_global_device_ids=true | all-gather | bytes 512000 | tf_op jit(solution)/shard_map/all_gather | solution.py:92
  74.6 2.0 bitcast_convert_fusion
  76.6 2.6 convolution_convert_fusion.7
  80.6 2.7 convolution_convert_fusion.1
  84.9 5.5 %fusion.5 = (f32[2,16,128]{2,1,0:T(8,128)S(1)}, bf16[2,16,128,384]{3,2,1,0:T(8,128)(2,1)}) fusion(f32[2,16,128,384]{3,2,1,0:T(8,128)} %copy-done.11, f32[2,16,128]{2,1,0:T(8,128)S(1)} %multiply_divide_fusion, pred[128,384]{1,0:T(8,128)(4,1)S(1)} %and_and_fusion, bf16[2,384,16,64]{1,3,2,0:T(8,128)(2,1)S(1)} %bitcast.123, ...), kind=kOutput, calls=%fused_computation.7 | convolution fusion | flops 212332544 | bytes 11616256 | tf_op jit(solution)/shard_map/transpose(jvp(mhqk,mkhd->mqhd))/dot_general | solution.py:76
  90.7 6.4 %convolution_convert_fusion.2 = bf16[2,16,384,64]{2,3,1,0:T(8,128)(2,1)S(1)} fusion(bf16[2,16,128,384]{3,2,1,0:T(8,128)(2,1)} %get-tuple-element.83, f32[2,16,128,384]{3,2,1,0:T(8,128)} %copy-done.11, f32[2,16,128]{2,1,0:T(8,128)S(1)} %neg.17, f32[2,16,128]{2,1,0:T(8,128)S(1)} %get-tuple-element.78, pred[128,384]{1,0:T(8,128)(4,1)S(1)} %and_and_fusion, ...), kind=kOutput, calls=%fused_computation.23 | convolution fusion | flops 213647360 | bytes 12156928 | tf_op jit(solution)/shard_map/transpose(jvp(mqhd,mkhd->mhqk))/dot_general | solution.py:65
  99.9 2.9 fusion.22
  104.1 11.8 %collective-permute-start.3 = (bf16[2,2,128,1024]{2,1,3,0:T(2,128)(2,1)}, bf16[2,2,128,1024]{2,1,3,0:T(2,128)(2,1)}, u32[]{:S(2)}, u32[]{:S(2)}) collective-permute-start(bf16[2,2,128,1024]{2,1,3,0:T(2,128)(2,1)} %get-tuple-element.69), channel_id=1, source_target_pairs={{0,1},{1,2},{2,3},{3,4},{4,5},{5,6},{6,7},{8,9},{9,10},{10,11},{11... | collective-permute-start | bytes 3145736 | tf_op jit(solution)/shard_map/ppermute | solution.py:30
  119.3 8.0 %fusion.18 = f32[2,16,8,8,128]{4,3,2,1,0:T(8,128)} fusion(bf16[2,384,16,64]{1,3,2,0:T(8,128)(2,1)} %bitcast.134, bf16[2,16,128,384]{3,2,1,0:T(8,128)(2,1)} %get-tuple-element.83, f32[2,16,128,384]{3,2,1,0:T(8,128)} %copy-done.11, f32[2,16,128]{2,1,0:T(8,128)S(1)} %neg.17, f32[2,16,128]{2,1,0:T(8,128)S(1)} %get-tuple-element.78, ...), kind=kOutput, calls=%fused_computation.39 | convolution fusion | flops 212860928 | bytes 12140544 | tf_op jit(solution)/shard_map/transpose(jvp(mqhd,mkhd->mhqk))/dot_general | solution.py:65
  128.3 55.9 %psum.21 = f32[]{:T(128)} all-reduce(f32[]{:T(128)S(6)} %sub.128), channel_id=1, replica_groups=mesh['member'=4,'token'=8] {'member','token'}, use_global_device_ids=true, to_apply=%region_8.9 | all-reduce | flops 1 | bytes 8 | tf_op jit(solution)/shard_map/psum | solution.py:171
  190.1 3.3 %add_convert_fusion = bf16[2,2,128,1024]{2,1,3,0:T(2,128)(2,1)S(1)} fusion(bf16[2,2,128,1024]{2,1,3,0:T(2,128)(2,1)} %collective-permute-done.3, bf16[2,2,128,1024]{2,1,3,0:T(2,128)(2,1)} %collective-permute-done.2, bf16[1,2,384,1024]{2,1,3,0:T(2,128)(2,1)S(1)} %copy.52, bf16[1,2,384,1024]{2,1,3,0:T(2,128)(2,1)S(1)} %copy-done.4), kind=kLoop, calls=%fused_computation.21 | loop fusion | flops 3670016 | bytes 6291456 | tf_op jit(solution)/shard_map/convert.5
  195.3 2.2 reshape.590
  197.5 2.5 convolution_convert_fusion.6
  204.0 29.7 %all-reduce.6 = f32[128,1024]{1,0:T(8,128)} all-reduce(bf16[128,1024]{1,0:T(8,128)(2,1)} %reduce-scatter.2.cloned.1.call-done), channel_id=1, replica_groups=mesh['member'=4,'token'=8] {'member'}, use_global_device_ids=true, to_apply=%region_14.15 | all-reduce | flops 131072 | bytes 786432 | tf_op jit(solution)/shard_map/psum | solution.py:198
  233.8 78.6 %all-reduce.5.cloned.1.call-done = f32[100,1024]{1,0:T(8,128)} async-done(((f32[100,1024]{1,0:T(8,128)}), f32[100,1024]{1,0:T(8,128)}) %all-reduce.5.cloned.1.call-update) | async-done | bytes 409616 | tf_op jit(solution)/shard_map/psum | solution.py:171
  (125 shorter events, 42.6 us)
Async XLA Ops:
  8.0 44.9 %copy-start = (bf16[1024,1024]{1,0:T(8,128)(2,1)S(1)}, bf16[1024,1024]{1,0:T(8,128)(2,1)}, u32[]{:S(2)}) copy-start(bf16[1024,1024]{1,0:T(8,128)(2,1)} %param.31) | copy-start | bytes 6291460
  8.0 196.0 %reduce-scatter.2.cloned.1.call-start = ((), (), s32[]{:S(2)}) async-start(), calls=%async_computation.1 | async-start | bytes 2359296 | tf_op jit(solution)/shard_map/reduce_scatter | solution.py:195
  14.0 4.0 %copy-start.24 = (bf16[2,128,1024]{2,1,0:T(8,128)(2,1)S(1)}, bf16[2,128,1024]{2,1,0:T(8,128)(2,1)}, u32[]{:S(2)}) copy-start(bf16[2,128,1024]{2,1,0:T(8,128)(2,1)} %copy-done.23) | copy-start | bytes 1572868
  20.4 10.9 %copy-start.27 = (s32[1024]{0:T(1024)S(1)}, s32[1024]{0:T(1024)}, u32[]{:S(2)}) copy-start(s32[1024]{0:T(1024)} %param.37) | copy-start | bytes 12292
  20.4 10.9 %copy-start.28 = (f32[1024]{0:T(1024)S(1)}, f32[1024]{0:T(1024)}, u32[]{:S(2)}) copy-start(f32[1024]{0:T(1024)} %param.35) | copy-start | bytes 12292
  25.9 12.5 %collective-permute-start.1 = (bf16[2,2,128,1024]{2,1,3,0:T(2,128)(2,1)}, bf16[2,2,128,1024]{2,1,3,0:T(2,128)(2,1)}, u32[]{:S(2)}, u32[]{:S(2)}) collective-permute-start(bf16[2,2,128,1024]{2,1,3,0:T(2,128)(2,1)} %pad_maximum_fusion.1), channel_id=1, source_target_pairs={{1,0},{2,1},{3,2},{4,3},{5,4},{6,5},{7,6},{9,8},{10,9},{11,10},{12... | collective-permute-start | bytes 3145736 | tf_op jit(solution)/shard_map/ppermute | solution.py:22
  27.2 11.2 %collective-permute-start = (bf16[2,2,128,1024]{2,1,3,0:T(2,128)(2,1)}, bf16[2,2,128,1024]{2,1,3,0:T(2,128)(2,1)}, u32[]{:S(2)}, u32[]{:S(2)}) collective-permute-start(bf16[2,2,128,1024]{2,1,3,0:T(2,128)(2,1)} %pad_maximum_fusion.1), channel_id=1, source_target_pairs={{0,1},{1,2},{2,3},{3,4},{4,5},{5,6},{6,7},{8,9},{9,10},{10,11},{11... | collective-permute-start | bytes 3145736 | tf_op jit(solution)/shard_map/ppermute | solution.py:19
  35.6 2.7 copy-start.29
  38.2 8.7 %copy-start.18 = (f32[256,16,64]{0,2,1:T(8,128)}, f32[256,16,64]{0,2,1:T(8,128)S(1)}, u32[]{:S(2)}) copy-start(f32[256,16,64]{0,2,1:T(8,128)S(1)} %get-tuple-element.77) | copy-start | bytes 3145732
  46.9 4.5 %copy-start.12 = (bf16[1,2,384,1024]{2,3,1,0:T(8,128)(2,1)}, bf16[1,2,384,1024]{2,3,1,0:T(8,128)(2,1)S(1)}, u32[]{:S(2)}) copy-start(bf16[1,2,384,1024]{2,3,1,0:T(8,128)(2,1)S(1)} %copy.45) | copy-start | bytes 4718596
  48.7 2.7 copy-start.11
  51.4 2.7 copy-start.2
  53.3 17.8 %copy-start.25 = (f32[100,1024]{1,0:T(8,128)S(1)}, f32[100,1024]{1,0:T(8,128)}, u32[]{:S(2)}) copy-start(f32[100,1024]{1,0:T(8,128)} %param.34) | copy-start | bytes 1228804
  54.1 18.6 %copy-start.16 = (bf16[2,128,1024]{2,1,0:T(8,128)(2,1)}, bf16[2,128,1024]{2,1,0:T(8,128)(2,1)S(1)}, u32[]{:S(2)}) copy-start(bf16[2,128,1024]{2,1,0:T(8,128)(2,1)S(1)} %fusion.14) | copy-start | bytes 1572868
  80.6 4.3 %copy-start.13 = (bf16[1,2,384,1024]{2,3,1,0:T(8,128)(2,1)S(1)}, bf16[1,2,384,1024]{2,3,1,0:T(8,128)(2,1)}, u32[]{:S(2)}) copy-start(bf16[1,2,384,1024]{2,3,1,0:T(8,128)(2,1)} %copy-done.12) | copy-start | bytes 4718596
  90.5 221.8 %all-reduce.5.cloned.1.call-start = ((), (), s32[]{:S(2)}) async-start(), calls=%async_computation.2 | async-start | bytes 851968 | tf_op jit(solution)/shard_map/psum | solution.py:171
  99.9 16.0 %copy-start.8 = (f32[8,100,128]{2,1,0:T(8,128)S(1)}, f32[8,100,128]{2,1,0:T(8,128)}, u32[]{:S(2)}) copy-start(f32[8,100,128]{2,1,0:T(8,128)} %copy-done.7) | copy-start | bytes 1228804
  102.8 87.3 %collective-permute-start.2 = (bf16[2,2,128,1024]{2,1,3,0:T(2,128)(2,1)}, bf16[2,2,128,1024]{2,1,3,0:T(2,128)(2,1)}, u32[]{:S(2)}, u32[]{:S(2)}) collective-permute-start(bf16[2,2,128,1024]{2,1,3,0:T(2,128)(2,1)} %get-tuple-element.68), channel_id=1, source_target_pairs={{1,0},{2,1},{3,2},{4,3},{5,4},{6,5},{7,6},{9,8},{10,9},{11,10},{12... | collective-permute-start | bytes 3145736 | tf_op jit(solution)/shard_map/ppermute | solution.py:30
  104.1 86.1 %collective-permute-start.3 = (bf16[2,2,128,1024]{2,1,3,0:T(2,128)(2,1)}, bf16[2,2,128,1024]{2,1,3,0:T(2,128)(2,1)}, u32[]{:S(2)}, u32[]{:S(2)}) collective-permute-start(bf16[2,2,128,1024]{2,1,3,0:T(2,128)(2,1)} %get-tuple-element.69), channel_id=1, source_target_pairs={{0,1},{1,2},{2,3},{3,4},{4,5},{5,6},{6,7},{8,9},{9,10},{10,11},{11... | collective-permute-start | bytes 3145736 | tf_op jit(solution)/shard_map/ppermute | solution.py:30
  119.3 8.0 %copy-start.17 = (bf16[2,128,1024]{2,1,0:T(8,128)(2,1)S(1)}, bf16[2,128,1024]{2,1,0:T(8,128)(2,1)}, u32[]{:S(2)}) copy-start(bf16[2,128,1024]{2,1,0:T(8,128)(2,1)} %copy-done.16) | copy-start | bytes 1572868
  184.8 3.7 %copy-start.19 = (bf16[1024,1024]{1,0:T(8,128)(2,1)S(1)}, bf16[1024,1024]{1,0:T(8,128)(2,1)}, u32[]{:S(2)}) copy-start(bf16[1024,1024]{1,0:T(8,128)(2,1)} %param.28) | copy-start | bytes 6291460
  186.7 3.5 %copy-start.4 = (bf16[1,2,384,1024]{2,1,3,0:T(2,128)(2,1)S(1)}, bf16[1,2,384,1024]{2,1,3,0:T(2,128)(2,1)}, u32[]{:S(2)}) copy-start(bf16[1,2,384,1024]{2,1,3,0:T(2,128)(2,1)} %copy-done.3) | copy-start | bytes 4718596
  195.3 4.7 %copy-start.10 = (f32[256,16,64]{0,2,1:T(8,128)S(1)}, f32[256,16,64]{0,2,1:T(8,128)}, u32[]{:S(2)}) copy-start(f32[256,16,64]{0,2,1:T(8,128)} %copy-done.9) | copy-start | bytes 3145732
  201.7 112.4 %copy-start.1 = (bf16[1024,1024]{1,0:T(8,128)(2,1)S(1)}, bf16[1024,1024]{1,0:T(8,128)(2,1)}, u32[]{:S(2)}) copy-start(bf16[1024,1024]{1,0:T(8,128)(2,1)} %param.31) | copy-start | bytes 6291460
  (14 other events, 23.8 us)
Sparse Core Ops, SparseCore 0:
  90.6 63.5 reduce-scatter.1
Sparse Core Ops, SparseCore 1:
  184.9 127.4 all-reduce.4

commit v2 on v1

--- a/solution.py
+++ b/solution.py
@@ -1,6 +1,10 @@
+import functools
+
 import jax
 import jax.numpy as jnp
 from jax import lax
+from jax.experimental import pallas as pl
+from jax.experimental.pallas import tpu as pltpu
 from jax.sharding import PartitionSpec as P
 
 HEADS = 16
@@ -114,6 +118,224 @@
     return share, slope
 
 
+CHUNKS = 8
+
+
+def reduce_kernel(
+    places, product, decoder, out, decoder_out, chunk_slot, member_send, member_recv,
+    decoder_send, decoder_recv, first_recv, *rest
+):
+    groups, bits = places
+    sends, recvs = rest[-2:]
+    rest = list(rest[:-2])
+    me, here = lax.axis_index("token"), lax.axis_index("member")
+    low_bits = min(bits, CHUNKS.bit_length() - 1)
+    chunks = 1 << low_bits
+    width = product.shape[-1]
+    half = width // 2
+    piece = width // groups
+    started = []
+
+    def flip(bit):
+        return me + (1 << bit) * (1 - 2 * (lax.div(me, 1 << bit) % 2))
+
+    def bit_of(bit):
+        return lax.div(me, 1 << bit) % 2
+
+    def across(low):
+        target = me
+        for bit in range(low_bits):
+            if low >> bit & 1:
+                target = target + (1 << bit) * (1 - 2 * bit_of(bit))
+        return target
+
+    def send(source, target, device):
+        index = len(started)
+        copy = pltpu.make_async_remote_copy(
+            src_ref=source, dst_ref=target, send_sem=sends.at[index], recv_sem=recvs.at[index],
+            device_id=device, device_id_type=pl.DeviceIdType.MESH,
+        )
+        copy.start()
+        started.append(copy)
+        return copy
+
+    barrier = pltpu.get_barrier_semaphore()
+    token_partners = [across(low) for low in range(1, chunks)]
+    token_partners += [flip(bit) for bit in range(low_bits, bits)]
+    for partner in token_partners:
+        pl.semaphore_signal(
+            barrier, inc=1, device_id={"token": partner}, device_id_type=pl.DeviceIdType.MESH
+        )
+    for ahead in range(1, groups):
+        pl.semaphore_signal(
+            barrier, inc=1, device_id={"member": lax.rem(here + ahead, groups)},
+            device_id_type=pl.DeviceIdType.MESH,
+        )
+    pl.semaphore_wait(barrier, len(token_partners) + groups - 1)
+
+    copy0 = send(product.at[:, 1 - bit_of(0)], first_recv, {"token": flip(0)})
+    lanes = []
+    for part, order in enumerate((range(1, bits), range(bits - 1, 0, -1))):
+        columns = pl.ds(part * half, half)
+        lanes.append(dict(columns=columns, order=list(order), low=part == 0, part=part))
+    blocks = 1 << (bits - 1)
+    mine0 = bit_of(0)
+
+    dec_send = decoder.at[:, 1 - mine0]
+    dec_recv = rest.pop(0)
+    dec_copy = send(dec_send, dec_recv, {"token": flip(0)})
+
+    copy0.wait_recv()
+    for lane in lanes:
+        columns = lane["columns"]
+        lane["value"] = lambda q, columns=columns: (
+            product[q, mine0, :, columns].astype(jnp.float32)
+            + first_recv[q, :, columns].astype(jnp.float32)
+        )
+    dec_copy.wait_recv()
+    decoder_value = lambda q, recv=dec_recv: decoder[q, mine0] + recv[q]
+
+    for step in range(bits - 1):
+        blocks //= 2
+        for lane in lanes:
+            bit = lane["order"][step]
+            mine = bit_of(bit)
+            place = (
+                (lambda q, b: 2 * q + b) if lane["low"] else (lambda q, b, n=blocks: b * n + q)
+            )
+            send_buf, keep, recv = rest.pop(0), rest.pop(0), rest.pop(0)
+            for q in range(blocks):
+                send_buf[q] = lane["value"](place(q, 1 - mine)).astype(jnp.bfloat16)
+            lane["copy"] = send(send_buf, recv, {"token": flip(bit)})
+            for q in range(blocks):
+                keep[q] = lane["value"](place(q, mine))
+            lane["value"] = lambda q, keep=keep, recv=recv: keep[q] + recv[q].astype(jnp.float32)
+        bit = step + 1
+        mine = bit_of(bit)
+        count = chunks >> (bit + 1) if bit < low_bits else 1
+        send_buf, keep, recv = rest.pop(0), rest.pop(0), rest.pop(0)
+        if bit < low_bits:
+            for q in range(count):
+                send_buf[q] = decoder_value(2 * q + 1 - mine)
+                keep[q] = decoder_value(2 * q + mine)
+        else:
+            send_buf[0] = decoder_value(0)
+            keep[0] = send_buf[0]
+        dec_copy = send(send_buf, recv, {"token": flip(bit)})
+        decoder_value = lambda q, keep=keep, recv=recv: keep[q] + recv[q]
+        for lane in lanes:
+            lane["copy"].wait_recv()
+        dec_copy.wait_recv()
+
+    own_total, own_decoder = rest.pop(0), rest.pop(0)
+    for lane in lanes:
+        total = lane["value"](0)
+        for index in range(groups // 2):
+            spot = lane["part"] * (groups // 2) + index
+            own_total[spot] = total[:, index * piece : (index + 1) * piece]
+            member_send[spot] = own_total[spot].astype(jnp.bfloat16)
+    total = decoder_value(0)
+    for index in range(groups):
+        own_decoder[index] = total[:, index * piece : (index + 1) * piece]
+    waits = []
+    for ahead in range(1, groups):
+        target = lax.rem(here + ahead, groups)
+        waits.append(send(member_send.at[target], member_recv.at[ahead - 1], {"member": target}))
+        waits.append(send(own_decoder.at[target], decoder_recv.at[ahead - 1], {"member": target}))
+    for copy in waits:
+        copy.wait_recv()
+    summed = own_total[here]
+    chunk = own_decoder[here]
+    for ahead in range(groups - 1):
+        summed = summed + member_recv[ahead].astype(jnp.float32)
+        chunk = chunk + decoder_recv[ahead]
+    gathered = rest.pop(0)
+    gathered[here] = summed.astype(jnp.bfloat16)
+    decoder_send[here] = chunk
+    back, dec_back = [], []
+    for ahead in range(1, groups):
+        target = lax.rem(here + ahead, groups)
+        dec_back.append(send(decoder_send.at[here], decoder_send.at[here], {"member": target}))
+        back.append(send(gathered.at[here], gathered.at[here], {"member": target}))
+    for copy in dec_back:
+        copy.wait_recv()
+    mine = lax.rem(me, chunks)
+    for index in range(groups):
+        chunk_slot[mine, :, index * piece : (index + 1) * piece] = decoder_send[index]
+    last = [
+        send(chunk_slot.at[mine], chunk_slot.at[mine], {"token": across(low)})
+        for low in range(1, chunks)
+    ]
+    for copy in back:
+        copy.wait_recv()
+    for index in range(groups):
+        out[:, index * piece : (index + 1) * piece] = gathered[index].astype(jnp.float32)
+    for copy in last:
+        copy.wait_recv()
+    decoder_out[...] = chunk_slot[...]
+    for copy in started:
+        copy.wait_send()
+
+
+def reduce_gradients(product, decoder):
+    count, groups = lax.axis_size("token"), lax.axis_size("member")
+    bits = count.bit_length() - 1
+    low_bits = min(bits, CHUNKS.bit_length() - 1)
+    chunks = 1 << low_bits
+    width = product.shape[1]
+    rows = product.shape[0] // count
+    piece, half = width // groups, width // 2
+    deep = -(-decoder.shape[0] // (8 * chunks)) * 8
+    padded = jnp.pad(decoder, ((0, deep * chunks - decoder.shape[0]), (0, 0)))
+    f32, bf16 = jnp.float32, jnp.bfloat16
+    scratch = [
+        pltpu.VMEM((chunks, deep, width), f32),
+        pltpu.VMEM((groups, rows, piece), bf16),
+        pltpu.VMEM((groups - 1, rows, piece), bf16),
+        pltpu.VMEM((groups, deep, piece), f32),
+        pltpu.VMEM((groups - 1, deep, piece), f32),
+        pltpu.VMEM((count // 2, rows, width), bf16),
+        pltpu.VMEM((chunks // 2, deep, width), f32),
+    ]
+    blocks = count // 2
+    copies = 2
+    for step in range(bits - 1):
+        blocks //= 2
+        for _ in range(2):
+            scratch += [
+                pltpu.VMEM((blocks, rows, half), bf16),
+                pltpu.VMEM((blocks, rows, half), f32),
+                pltpu.VMEM((blocks, rows, half), bf16),
+            ]
+        left = max(chunks >> (step + 2), 1)
+        scratch += [pltpu.VMEM((left, deep, width), f32)] * 3
+        copies += 3
+    scratch += [
+        pltpu.VMEM((groups, rows, piece), f32),
+        pltpu.VMEM((groups, deep, piece), f32),
+        pltpu.VMEM((groups, rows, piece), bf16),
+    ]
+    copies += 4 * (groups - 1) + chunks - 1
+    scratch += [pltpu.SemaphoreType.DMA((copies,)), pltpu.SemaphoreType.DMA((copies,))]
+    out, whole = pl.pallas_call(
+        functools.partial(reduce_kernel, (groups, bits)),
+        out_shape=(
+            jax.ShapeDtypeStruct((rows, width), f32),
+            jax.ShapeDtypeStruct((chunks, deep, width), f32),
+        ),
+        in_specs=[pl.BlockSpec(memory_space=pltpu.VMEM)] * 2,
+        out_specs=[pl.BlockSpec(memory_space=pltpu.VMEM)] * 2,
+        scratch_shapes=scratch,
+        compiler_params=pltpu.CompilerParams(
+            collective_id=0, has_side_effects=True, vmem_limit_bytes=40 * 2**20
+        ),
+    )(
+        product.reshape(count // 2, 2, rows, width),
+        padded.reshape(chunks // 2, 2, deep, width),
+    )
+    return out, whole.reshape(chunks * deep, width)
+
+
 def shards(
     members_in,
     member_noise,
@@ -168,10 +390,6 @@
     carried_slope = jnp.einsum(
         "mvt,vc->mtc", slope, decoder_projection_weight, preferred_element_type=jnp.float32
     ).astype(jnp.bfloat16)
-    overall_scoring_amount, grad_decoder = lax.psum((share, decoder_piece), ("member", "token"))
-    mean_scoring = overall_scoring_amount / (
-        observations.shape[0] * observations.shape[1] * lax.axis_size("token")
-    )
     flat_grad = carried_slope.reshape(member_rows * tokens, width)
     grad_attended = (
         jnp.dot(flat_grad, weight_out.T, preferred_element_type=jnp.float32)
@@ -192,10 +410,13 @@
     grad_members = (grad_front + carried_slope.astype(jnp.float32)).astype(jnp.bfloat16)
     contract = (((0,), (0,)), ((), ()))
     product = lax.dot_general(flat_att, flat_grad, contract, preferred_element_type=jnp.float32)
-    scattered = lax.psum_scatter(
-        product.astype(jnp.bfloat16), "token", scatter_dimension=0, tiled=True
-    )
-    grad_out = lax.psum(scattered.astype(jnp.float32), "member")
+    variables = decoder_piece.shape[0]
+    decoder_piece = jnp.concatenate([decoder_piece, jnp.full((1, width), share)])
+    grad_out, decoder_sum = reduce_gradients(product.astype(jnp.bfloat16), decoder_piece)
+    grad_decoder = decoder_sum[:variables]
+    mean_scoring = decoder_sum[variables, 0] / (
+        observations.shape[0] * observations.shape[1] * lax.axis_size("token")
+    )
     return (mean_scoring, grad_members, grad_out, grad_decoder)
 
 

time: 324 us -> 193 us (0.60)
  blocking collectives: 102 us -> 16.3 us
  waiting for transfers between devices: 78.6 us -> 0.01 us
  Pallas kernels: 0 us -> 58.5 us
  between operations: 20 us -> 5.28 us
  matrix products: 47.5 us -> 37 us
    psum x2 -> x0, blocking collectives: 85.6 us -> none  [the longest x1 55.9 us: shards(): lax.psum((share, decoder_piece), ('member', 'token'))]
    psum x1 -> x0, waiting for transfers between devices: 78.6 us -> none  [shards(): lax.psum((share, decoder_piece), ('member', 'token'))]
    pallas_call x0 -> x1, Pallas kernels: none -> 58.5 us  [reduce_gradients(): pl.pallas_call(functools.partial(reduce_kernel, (groups, bits)), out_shap...]
    dot_general x3, matrix products: 16.2 us -> 8.98 us  [attend(): jnp.einsum('mqhd,mkhd->mhqk', query_heads, key_heads, preferred_element_t...]
    unnamed x67 -> x83, local copies, waits for them, and re-layouts: 15.6 us -> 14.9 us
  transfers between devices with their start and end apart: 6 -> 4, of which waited for: 1 -> 0; matrix products, arithmetic and copies ran while one was open for 14% -> 7% of each run, Pallas kernels for 0% -> 30%
where the time goes in v2:
time: 193 us; the launch traced here: 192 us
  Pallas kernels  58.5 us (30%)
  matrix products  37 us (19%)
  local copies, waits for them, and re-layouts  29.2 us (15%)
  other arithmetic  27.4 us (14%)
  starting transfers between devices  18.3 us (9%)
  blocking collectives  16.3 us (8%)
  between operations  5.28 us (3%)
    pallas_call x1, Pallas kernels, reduce_gradients(): pl.pallas_call(functools.partial(reduce_kernel, (groups, bits)), out_shap...  58.5 us
    all_gather x1, blocking collectives, score_and_slope(): everyone = lax.all_gather(own, 'member', axis=0, tiled=True)  16.3 us
    unnamed x83, local copies, waits for them, and re-layouts  14.9 us
    ppermute x2, starting transfers between devices, from_behind(): return lax.ppermute(block, axis, route)  13 us
    dot_general x3, matrix products, attend(): jnp.einsum('mqhd,mkhd->mhqk', query_heads, key_heads, preferred_element_t...  8.98 us
    dot_general x3, matrix products, attend(): jnp.einsum('mhqk,mkhd->mqhd', probs, value_heads, preferred_element_type=...  8.72 us
    concatenate x1, other arithmetic, extended_2(): block = jnp.concatenate([low, block, high], axis=dim)  5.75 us
    dot_general x2, matrix products, project(): jnp.dot(flat, weight_value, preferred_element_type=jnp.float32)  5.02 us
  transfers between devices with their start and end apart: 4, of which 0 were waited for; matrix products, arithmetic and copies ran while one was open for 7% of the time, Pallas kernels for 30%

profile of v2, /device:TPU:0, one launch (start us, length us, event | category | flops | bytes accessed | tf_op | source)
XLA Modules:
  0.0 191.9 jit_solution(4150809308049339740)
XLA Ops:
  3.7 2.5 %convolution_convert_fusion.8 = bf16[256,1024]{1,0:T(8,128)(2,1)S(1)} fusion(bf16[256,1024]{1,0:T(8,128)(2,1)S(1)} %bitcast.148, bf16[1024,1024]{1,0:T(8,128)(2,1)} %param.30), kind=kOutput, calls=%fused_computation.35 | convolution fusion | flops 537133056 | bytes 3145728 | tf_op jit(solution)/shard_map/jvp()/dot_general | solution.py:57
  6.6 4.0 %copy.43 = bf16[1024,1024]{0,1:T(8,128)(2,1)} copy(bf16[1024,1024]{1,0:T(8,128)(2,1)} %param.29) | data formatting | bytes 4194304 | tf_op args[4]
  10.6 2.3 %multiply_reduce_fusion.2 = (f32[256,16]{0,1:T(8,128)S(1)}, f32[256,16,64]{0,2,1:T(8,128)S(1)}) fusion(bf16[256,1024,1]{1,0,2:T(8,128)(2,1)S(1)} %bitcast.150, bf16[16,64,1024]{2,1,0:T(8,128)(2,1)} %bitcast.141), kind=kOutput, calls=%fused_computation.64 | convolution fusion | flops 537391104 | bytes 3686400 | tf_op jit(solution)/shard_map/jvp()/dot_general | solution.py:54
  16.1 2.5 %pad_maximum_fusion.1 = bf16[2,2,128,1024]{2,1,3,0:T(2,128)(2,1)} fusion(bf16[1,2,128,1024]{2,1,3,0:T(2,128)(2,1)S(1)} %copy.44, bf16[1,2,128,1024]{2,1,3,0:T(2,128)(2,1)S(1)} %convert_element_type.167), kind=kLoop, calls=%fused_computation.55 | loop fusion | flops 524288 | bytes 2097152 | tf_op jit(solution)/shard_map/stack | solution.py:361
  19.9 4.0 %collective-permute-start = (bf16[2,2,128,1024]{2,1,3,0:T(2,128)(2,1)}, bf16[2,2,128,1024]{2,1,3,0:T(2,128)(2,1)}, u32[]{:S(2)}, u32[]{:S(2)}) collective-permute-start(bf16[2,2,128,1024]{2,1,3,0:T(2,128)(2,1)} %pad_maximum_fusion.1), channel_id=1, source_target_pairs={{0,1},{1,2},{2,3},{3,4},{4,5},{5,6},{6,7},{8,9},{9,10},{10,11},{11... | collective-permute-start | bytes 3145736 | tf_op jit(solution)/shard_map/ppermute | solution.py:23
  24.4 4.0 %copy.46 = bf16[1024,1024]{0,1:T(8,128)(2,1)} copy(bf16[1024,1024]{1,0:T(8,128)(2,1)} %param.28) | data formatting | bytes 4194304 | tf_op args[3]
  28.3 2.5 %multiply_reduce_fusion.1 = (f32[256,16]{0,1:T(8,128)S(1)}, f32[256,16,64]{0,2,1:T(8,128)S(1)}) fusion(bf16[256,1024,1]{1,0,2:T(8,128)(2,1)} %bitcast.149, bf16[16,64,1024]{2,1,0:T(8,128)(2,1)} %bitcast.140), kind=kOutput, calls=%fused_computation.62 | convolution fusion | flops 537391104 | bytes 3686400 | tf_op jit(solution)/shard_map/jvp()/dot_general | solution.py:51
  31.2 5.7 %pad_maximum_fusion = bf16[2,2,384,1024]{2,1,3,0:T(2,128)(2,1)S(1)} fusion(bf16[2,2,128,1024]{2,1,3,0:T(2,128)(2,1)} %collective-permute-done.1, bf16[1,2,128,1024]{2,1,3,0:T(2,128)(2,1)S(1)} %copy.44, bf16[1,2,128,1024]{2,1,3,0:T(2,128)(2,1)S(1)} %convert_element_type.167, bf16[2,2,128,1024]{2,1,3,0:T(2,128)(2,1)} %collective-permute-done), kind=kLoop, calls=%fused_computation.13 | loop fusion | flops 12582912 | bytes 6291456 | tf_op jit(solution)/shard_map/concatenate | solution.py:27
  36.9 2.2 %fusion.78 = (bf16[1,2,384,1024]{2,1,3,0:T(2,128)(2,1)S(1)}, bf16[1,2,384,1024]{2,1,3,0:T(2,128)(2,1)S(1)}) fusion(bf16[2,2,384,1024]{2,1,3,0:T(2,128)(2,1)S(1)} %pad_maximum_fusion), kind=kLoop, calls=%fused_computation.167 | loop fusion | bytes 6291456 | tf_op jit(solution)/shard_map/jvp()/slice | solution.py:367
  39.6 1.8 fusion.7
  41.4 2.6 %copy-done.12 = f32[2,16,128,384]{3,2,1,0:T(8,128)} copy-done((f32[2,16,128,384]{3,2,1,0:T(8,128)}, f32[2,16,128,384]{3,2,1,0:T(8,128)S(1)}, u32[]{:S(2)}) %copy-start.12) | copy-done | bytes 6291480
  48.5 16.3 %all_gather.3 = f32[8,100,128]{2,1,0:T(8,128)S(1)} all-gather(f32[2,100,128]{2,1,0:T(8,128)S(1)} %fusion.21), channel_id=1, replica_groups=mesh['member'=4,'token'=8] {'member'}, dimensions={0}, use_global_device_ids=true | all-gather | bytes 512000 | tf_op jit(solution)/shard_map/all_gather | solution.py:96
  71.2 2.0 %copy.50 = bf16[256,1024]{0,1:T(8,128)(2,1)} copy(bf16[256,1024]{1,0:T(8,128)(2,1)} %convolution_convert_fusion.7) | data formatting | bytes 1048576 | tf_op jit(solution)/shard_map/convert_element_type | solution.py:396
  74.5 2.7 %convolution_convert_fusion.1 = bf16[2,16,64,384]{3,2,1,0:T(8,128)(2,1)S(1)} fusion(bf16[2,16,128,384]{3,2,1,0:T(8,128)(2,1)} %copy-done.2, bf16[2,16,64,128]{3,0,2,1:T(2,128)(2,1)S(1)} %bitcast.138), kind=kOutput, calls=%fused_computation.22 | convolution fusion | flops 202113024 | bytes 5242880 | tf_op jit(solution)/shard_map/transpose(jvp(mhqk,mkhd->mqhd))/dot_general | solution.py:80
  77.3 4.5 %fusion.5 = (f32[2,16,128]{2,1,0:T(8,128)S(1)}, bf16[2,16,128,384]{3,2,1,0:T(8,128)(2,1)S(1)}) fusion(f32[2,16,128,384]{3,2,1,0:T(8,128)} %copy-done.12, f32[2,16,128]{2,1,0:T(8,128)S(1)} %multiply_divide_fusion, pred[128,384]{1,0:T(8,128)(4,1)S(1)} %and_and_fusion, bf16[2,384,16,64]{1,3,2,0:T(8,128)(2,1)S(1)} %bitcast.133, ...), kind=kOutput, calls=%fused_computation.7 | convolution fusion | flops 212332544 | bytes 11616256 | tf_op jit(solution)/shard_map/transpose(jvp(mhqk,mkhd->mqhd))/dot_general | solution.py:80
  81.9 4.1 %fusion.18 = f32[2,16,8,8,128]{4,3,2,1,0:T(8,128)} fusion(bf16[2,384,16,64]{1,3,2,0:T(8,128)(2,1)S(1)} %bitcast.144, bf16[2,16,128,384]{3,2,1,0:T(8,128)(2,1)S(1)} %get-tuple-element.87, f32[2,16,128,384]{3,2,1,0:T(8,128)S(1)} %bitcast.131, f32[2,16,128]{2,1,0:T(8,128)S(1)} %neg.17, f32[2,16,128]{2,1,0:T(8,128)S(1)} %get-tuple-element.82, ...), kind=kOutput, calls=%fused_computation.39 | convolution fusion | flops 212860928 | bytes 12140544 | tf_op jit(solution)/shard_map/transpose(jvp(mqhd,mkhd->mhqk))/dot_general | solution.py:69
  86.0 3.1 %convolution_convert_fusion.2 = bf16[2,16,384,64]{2,3,1,0:T(8,128)(2,1)S(1)} fusion(bf16[2,16,128,384]{3,2,1,0:T(8,128)(2,1)S(1)} %get-tuple-element.87, f32[2,16,128,384]{3,2,1,0:T(8,128)S(1)} %bitcast.131, f32[2,16,128]{2,1,0:T(8,128)S(1)} %neg.17, f32[2,16,128]{2,1,0:T(8,128)S(1)} %get-tuple-element.82, pred[128,384]{1,0:T(8,128)(4,1)S(1)} %and_and_fusion, ...), kind=kOutput, calls=%fused_computation.23 | convolution fusion | flops 213647360 | bytes 12156928 | tf_op jit(solution)/shard_map/transpose(jvp(mqhd,mkhd->mhqk))/dot_general | solution.py:69
  93.1 3.0 %fusion.22 = (bf16[2,2,128,1024]{2,1,3,0:T(2,128)(2,1)}, bf16[2,2,128,1024]{2,1,3,0:T(2,128)(2,1)}) fusion(bf16[1,2,384,1024]{2,1,3,0:T(2,128)(2,1)S(1)} %copy.52, bf16[1,2,384,1024]{2,1,3,0:T(2,128)(2,1)S(1)} %copy.55), kind=kLoop, calls=%fused_computation.47 | loop fusion | flops 4194304 | bytes 5242880 | tf_op jit(solution)/shard_map/transpose(jvp())/add_any | solution.py:367
  97.3 11.8 %collective-permute-start.3 = (bf16[2,2,128,1024]{2,1,3,0:T(2,128)(2,1)}, bf16[2,2,128,1024]{2,1,3,0:T(2,128)(2,1)}, u32[]{:S(2)}, u32[]{:S(2)}) collective-permute-start(bf16[2,2,128,1024]{2,1,3,0:T(2,128)(2,1)} %get-tuple-element.73), channel_id=1, source_target_pairs={{0,1},{1,2},{2,3},{3,4},{4,5},{5,6},{6,7},{8,9},{9,10},{10,11},{11... | collective-permute-start | bytes 3145736 | tf_op jit(solution)/shard_map/ppermute | solution.py:34
  113.7 58.5 %shard_map.166 = (f32[128,1024]{1,0:T(8,128)S(1)}, f32[8,16,1024]{2,1,0:T(8,128)S(1)}) custom-call(bf16[4,2,128,1024]{3,2,1,0:T(8,128)(2,1)S(1)} %bitcast.126, f32[4,2,16,1024]{3,2,1,0:T(8,128)S(1)} %bitcast.127), custom_call_target="tpu_custom_call" | custom-call | tf_op jit(solution)/shard_map/pallas_call | solution.py:320
  176.2 3.2 %add_convert_fusion = bf16[2,2,128,1024]{2,1,3,0:T(2,128)(2,1)S(1)} fusion(bf16[2,2,128,1024]{2,1,3,0:T(2,128)(2,1)} %collective-permute-done.3, bf16[2,2,128,1024]{2,1,3,0:T(2,128)(2,1)} %collective-permute-done.2, bf16[1,2,384,1024]{2,1,3,0:T(2,128)(2,1)S(1)} %copy-done.4, bf16[1,2,384,1024]{2,1,3,0:T(2,128)(2,1)S(1)} %copy-done.6), kind=kLoop, calls=%fused_computation.21 | loop fusion | flops 3670016 | bytes 6291456 | tf_op jit(solution)/shard_map/convert.5
  179.4 1.9 slice_convert_fusion
  181.3 2.2 %reshape.604 = f32[256,16,64]{0,2,1:T(8,128)S(1)} reshape(f32[1,2,128,1024]{2,1,3,0:T(2,128)} %get-tuple-element.76) | data formatting | bytes 2097152 | tf_op jit(solution)/shard_map/transpose(jvp())/convert_element_type | solution.py:54
  183.4 2.5 %convolution_convert_fusion.6 = bf16[256,1024]{1,0:T(8,128)(2,1)S(1)} fusion(bf16[1024,1024]{1,0:T(8,128)(2,1)} %param.30, bf16[128,8,2,128]{3,2,1,0:T(2,128)(2,1)} %bitcast.146), kind=kOutput, calls=%fused_computation.33 | convolution fusion | flops 537133056 | bytes 3145728 | tf_op jit(solution)/shard_map/transpose(jvp())/dot_general | solution.py:57
  (138 shorter events, 36.7 us)
Async XLA Ops:
  0.6 46.4 %copy-start = (bf16[1024,1024]{1,0:T(8,128)(2,1)S(1)}, bf16[1024,1024]{1,0:T(8,128)(2,1)}, u32[]{:S(2)}) copy-start(bf16[1024,1024]{1,0:T(8,128)(2,1)} %param.31) | copy-start | bytes 6291460
  6.6 4.0 %copy-start.30 = (bf16[2,128,1024]{2,1,0:T(8,128)(2,1)S(1)}, bf16[2,128,1024]{2,1,0:T(8,128)(2,1)}, u32[]{:S(2)}) copy-start(bf16[2,128,1024]{2,1,0:T(8,128)(2,1)} %copy-done.29) | copy-start | bytes 1572868
  13.0 10.9 %copy-start.33 = (s32[1024]{0:T(1024)S(1)}, s32[1024]{0:T(1024)}, u32[]{:S(2)}) copy-start(s32[1024]{0:T(1024)} %param.37) | copy-start | bytes 12292
  13.0 10.9 %copy-start.34 = (f32[1024]{0:T(1024)S(1)}, f32[1024]{0:T(1024)}, u32[]{:S(2)}) copy-start(f32[1024]{0:T(1024)} %param.35) | copy-start | bytes 12292
  18.6 12.5 %collective-permute-start.1 = (bf16[2,2,128,1024]{2,1,3,0:T(2,128)(2,1)}, bf16[2,2,128,1024]{2,1,3,0:T(2,128)(2,1)}, u32[]{:S(2)}, u32[]{:S(2)}) collective-permute-start(bf16[2,2,128,1024]{2,1,3,0:T(2,128)(2,1)} %pad_maximum_fusion.1), channel_id=1, source_target_pairs={{1,0},{2,1},{3,2},{4,3},{5,4},{6,5},{7,6},{9,8},{10,9},{11,10},{12... | collective-permute-start | bytes 3145736 | tf_op jit(solution)/shard_map/ppermute | solution.py:26
  19.9 11.3 %collective-permute-start = (bf16[2,2,128,1024]{2,1,3,0:T(2,128)(2,1)}, bf16[2,2,128,1024]{2,1,3,0:T(2,128)(2,1)}, u32[]{:S(2)}, u32[]{:S(2)}) collective-permute-start(bf16[2,2,128,1024]{2,1,3,0:T(2,128)(2,1)} %pad_maximum_fusion.1), channel_id=1, source_target_pairs={{0,1},{1,2},{2,3},{3,4},{4,5},{5,6},{6,7},{8,9},{9,10},{10,11},{11... | collective-permute-start | bytes 3145736 | tf_op jit(solution)/shard_map/ppermute | solution.py:23
  30.9 8.7 %copy-start.20 = (f32[256,16,64]{0,2,1:T(8,128)}, f32[256,16,64]{0,2,1:T(8,128)S(1)}, u32[]{:S(2)}) copy-start(f32[256,16,64]{0,2,1:T(8,128)S(1)} %get-tuple-element.81) | copy-start | bytes 3145732
  39.6 5.9 %copy-start.13 = (bf16[1,2,384,1024]{2,3,1,0:T(8,128)(2,1)}, bf16[1,2,384,1024]{2,3,1,0:T(8,128)(2,1)S(1)}, u32[]{:S(2)}) copy-start(bf16[1,2,384,1024]{2,3,1,0:T(8,128)(2,1)S(1)} %copy.45) | copy-start | bytes 4718596
  47.0 18.2 %copy-start.18 = (bf16[2,16,64,128]{3,2,1,0:T(8,128)(2,1)}, bf16[2,16,64,128]{3,2,1,0:T(8,128)(2,1)S(1)}, u32[]{:S(2)}) copy-start(bf16[2,16,64,128]{3,2,1,0:T(8,128)(2,1)S(1)} %convolution_convert_fusion.5) | copy-start | bytes 1572868
  47.4 17.8 %copy-start.31 = (f32[100,1024]{1,0:T(8,128)S(1)}, f32[100,1024]{1,0:T(8,128)}, u32[]{:S(2)}) copy-start(f32[100,1024]{1,0:T(8,128)} %param.34) | copy-start | bytes 1228804
  73.2 4.0 %copy-start.14 = (bf16[1,2,384,1024]{2,3,1,0:T(8,128)(2,1)S(1)}, bf16[1,2,384,1024]{2,3,1,0:T(8,128)(2,1)}, u32[]{:S(2)}) copy-start(bf16[1,2,384,1024]{2,3,1,0:T(8,128)(2,1)} %copy-done.13) | copy-start | bytes 4718596
  74.5 7.3 %slice-start = ((s8[6291456]{0:T(1024)(128)(4,1)}), s8[4194304]{0:T(1024)(128)(4,1)S(1)}, s32[]{:S(2)}) async-start(s8[6291456]{0:T(1024)(128)(4,1)} %bitcast.130), calls=%async_computation | async-start | bytes 8388608
  77.3 4.5 %slice-start.1 = ((s8[6291456]{0:T(1024)(128)(4,1)}), s8[2097152]{0:T(1024)(128)(4,1)S(1)}, s32[]{:S(2)}) async-start(s8[6291456]{0:T(1024)(128)(4,1)} %bitcast.130), calls=%async_computation.1 | async-start | bytes 4194304
  77.3 4.5 %copy-start.27 = (bf16[1,2,384,1024]{2,3,1,0:T(8,128)(2,1)S(1)}, bf16[1,2,384,1024]{2,3,1,0:T(8,128)(2,1)}, u32[]{:S(2)}) copy-start(bf16[1,2,384,1024]{2,3,1,0:T(8,128)(2,1)} %copy-done.26) | copy-start | bytes 4718596
  81.9 4.1 %copy-start.21 = (f32[256,16,64]{0,2,1:T(8,128)S(1)}, f32[256,16,64]{0,2,1:T(8,128)}, u32[]{:S(2)}) copy-start(f32[256,16,64]{0,2,1:T(8,128)} %copy-done.20) | copy-start | bytes 3145732
  86.0 3.1 %copy-start.16 = (bf16[2,128,1024]{2,1,0:T(8,128)(2,1)S(1)}, bf16[2,128,1024]{2,1,0:T(8,128)(2,1)}, u32[]{:S(2)}) copy-start(bf16[2,128,1024]{2,1,0:T(8,128)(2,1)} %copy-done.15) | copy-start | bytes 1572868
  86.0 3.1 %copy-start.19 = (bf16[2,16,64,128]{3,2,1,0:T(8,128)(2,1)S(1)}, bf16[2,16,64,128]{3,2,1,0:T(8,128)(2,1)}, u32[]{:S(2)}) copy-start(bf16[2,16,64,128]{3,2,1,0:T(8,128)(2,1)} %copy-done.18) | copy-start | bytes 1572868
  91.4 4.6 %copy-start.3 = (bf16[1,2,384,1024]{2,1,3,0:T(2,128)(2,1)}, bf16[1,2,384,1024]{2,1,3,0:T(2,128)(2,1)S(1)}, u32[]{:S(2)}) copy-start(bf16[1,2,384,1024]{2,1,3,0:T(2,128)(2,1)S(1)} %copy.52) | copy-start | bytes 4718596
  96.0 80.1 %collective-permute-start.2 = (bf16[2,2,128,1024]{2,1,3,0:T(2,128)(2,1)}, bf16[2,2,128,1024]{2,1,3,0:T(2,128)(2,1)}, u32[]{:S(2)}, u32[]{:S(2)}) collective-permute-start(bf16[2,2,128,1024]{2,1,3,0:T(2,128)(2,1)} %get-tuple-element.72), channel_id=1, source_target_pairs={{1,0},{2,1},{3,2},{4,3},{5,4},{6,5},{7,6},{9,8},{10,9},{11,10},{12... | collective-permute-start | bytes 3145736 | tf_op jit(solution)/shard_map/ppermute | solution.py:34
  97.3 78.8 %collective-permute-start.3 = (bf16[2,2,128,1024]{2,1,3,0:T(2,128)(2,1)}, bf16[2,2,128,1024]{2,1,3,0:T(2,128)(2,1)}, u32[]{:S(2)}, u32[]{:S(2)}) collective-permute-start(bf16[2,2,128,1024]{2,1,3,0:T(2,128)(2,1)} %get-tuple-element.73), channel_id=1, source_target_pairs={{0,1},{1,2},{2,3},{3,4},{4,5},{5,6},{6,7},{8,9},{9,10},{10,11},{11... | collective-permute-start | bytes 3145736 | tf_op jit(solution)/shard_map/ppermute | solution.py:34
  112.5 61.7 %copy-start.22 = (f32[256,16,64]{0,2,1:T(8,128)S(1)}, f32[256,16,64]{0,2,1:T(8,128)}, u32[]{:S(2)}) copy-start(f32[256,16,64]{0,2,1:T(8,128)} %copy-done.20) | copy-start | bytes 3145732
  112.5 61.7 %copy-start.23 = (f32[2,16,8,8,128]{4,3,2,1,0:T(8,128)S(1)}, f32[2,16,8,8,128]{4,3,2,1,0:T(8,128)}, u32[]{:S(2)}) copy-start(f32[2,16,8,8,128]{4,3,2,1,0:T(8,128)} %fusion.18) | copy-start | bytes 3145732
  181.3 4.7 %copy-start.11 = (f32[256,16,64]{0,2,1:T(8,128)S(1)}, f32[256,16,64]{0,2,1:T(8,128)}, u32[]{:S(2)}) copy-start(f32[256,16,64]{0,2,1:T(8,128)} %copy-done.10) | copy-start | bytes 3145732
  187.7 3.1 %copy-start.1 = (bf16[1024,1024]{1,0:T(8,128)(2,1)S(1)}, bf16[1024,1024]{1,0:T(8,128)(2,1)}, u32[]{:S(2)}) copy-start(bf16[1024,1024]{1,0:T(8,128)(2,1)} %param.31) | copy-start | bytes 6291460
  (20 other events, 39.5 us)

commit v3 on v2

--- a/solution.py
+++ b/solution.py
@@ -13,19 +13,6 @@
 
 EPSILON = 1e-06
 SMOOTH = 0.01
-
-
-def extended_2(block, sides, width):
-    for axis, dim in sides:
-        count = lax.axis_size(axis)
-        forward = [(i, i + 1) for i in range(count - 1)]
-        backward = [(target, source) for source, target in forward]
-        low = lax.ppermute(
-            lax.slice_in_dim(block, block.shape[dim] - width, None, axis=dim), axis, forward
-        )
-        high = lax.ppermute(lax.slice_in_dim(block, 0, width, axis=dim), axis, backward)
-        block = jnp.concatenate([low, block, high], axis=dim)
-    return block
 
 
 def from_behind(block, axis, distance):
@@ -59,26 +46,119 @@
     return (query.reshape(full_shape), key.reshape(full_shape), value.reshape(full_shape))
 
 
-def attend(query, keys, values, leading_realization, total):
-    member_rows, queries, width = query.shape
-    realization_number = keys.shape[1]
+LANES = 256
+
+
+def lane_pairs(depth):
+    lane = lax.broadcasted_iota(jnp.int32, (1, 128), 1)
+    return [(lane >= first) & (lane < first + depth) for first in range(0, 128, depth)]
+
+
+def allowed_keys(tokens):
+    index, count = lax.axis_index("token"), lax.axis_size("token")
+    row = lax.broadcasted_iota(jnp.int32, (tokens, 3 * tokens), 0)
+    column = lax.broadcasted_iota(jnp.int32, (tokens, 3 * tokens), 1)
+    least = jnp.where(index == 0, tokens, 0)
+    most = jnp.where(index == count - 1, 2 * tokens, 3 * tokens)
+    window = (column >= row) & (column < row + 2 * HALF)
+    return window & (column >= least) & (column < most)
+
+
+def product_of(left, right, left_dim, right_dim):
+    return lax.dot_general(
+        left, right, (((left_dim,), (right_dim,)), ((), ())), preferred_element_type=jnp.float32
+    )
+
+
+def raised_of(query, keys, allowed, scale):
+    raised = jnp.where(allowed, jnp.exp(product_of(query, keys, 1, 1) * scale), 0.0)
+    return raised / jnp.sum(raised, axis=-1, keepdims=True)
+
+
+def attend_kernel(depth, query, below, own, above, out):
+    tokens = query.shape[1]
+    allowed = allowed_keys(tokens)
+    scale = depth**-0.5
+    for first in range(0, LANES, 128):
+        lanes = slice(first, first + 128)
+        keys, values = (
+            jnp.concatenate([block[kind, 0, :, lanes] for block in (below, own, above)], axis=0)
+            for kind in (0, 1)
+        )
+        mixed = jnp.zeros((tokens, 128), jnp.float32)
+        for chosen in lane_pairs(depth):
+            picked = jnp.where(chosen, query[0, :, lanes], 0)
+            probs = raised_of(picked, keys, allowed, scale).astype(jnp.bfloat16)
+            mixed = jnp.where(chosen, product_of(probs, values, 1, 0), mixed)
+        out[0, :, lanes] = mixed.astype(jnp.bfloat16)
+
+
+def attend_back_kernel(
+    depth, query, below, own, above, slope, query_out, below_out, own_out, above_out
+):
+    tokens = query.shape[1]
+    allowed = allowed_keys(tokens)
+    scale = depth**-0.5
+    for first in range(0, LANES, 128):
+        lanes = slice(first, first + 128)
+        keys, values = (
+            jnp.concatenate([block[kind, 0, :, lanes] for block in (below, own, above)], axis=0)
+            for kind in (0, 1)
+        )
+        query_slope = jnp.zeros((tokens, 128), jnp.float32)
+        key_slope = jnp.zeros((3 * tokens, 128), jnp.float32)
+        value_slope = jnp.zeros((3 * tokens, 128), jnp.float32)
+        for chosen in lane_pairs(depth):
+            picked = jnp.where(chosen, query[0, :, lanes], 0)
+            pulled = jnp.where(chosen, slope[0, :, lanes], 0)
+            probs = raised_of(picked, keys, allowed, scale)
+            weight = product_of(pulled, values, 1, 1)
+            mean = jnp.sum(weight * probs, axis=-1, keepdims=True)
+            score_slope = (probs * (weight - mean) * scale).astype(jnp.bfloat16)
+            query_slope = jnp.where(chosen, product_of(score_slope, keys, 1, 0), query_slope)
+            key_slope = key_slope + product_of(score_slope, picked, 0, 0)
+            value_slope = value_slope + product_of(probs.astype(jnp.bfloat16), pulled, 0, 0)
+        query_out[0, :, lanes] = query_slope.astype(jnp.bfloat16)
+        for kind, total in ((0, key_slope), (1, value_slope)):
+            below_out[kind, 0, :, lanes] = total[:tokens].astype(jnp.bfloat16)
+            own_out[kind, 0, :, lanes] = total[tokens : 2 * tokens]
+            above_out[kind, 0, :, lanes] = total[2 * tokens :].astype(jnp.bfloat16)
+
+
+def attention(query, below, own, above, slope=None):
+    members, tokens, width = query.shape
+    assert tokens == HALF
     depth = width // HEADS
-    query_heads = query.reshape(member_rows, queries, HEADS, depth)
-    key_heads = keys.reshape(member_rows, realization_number, HEADS, depth)
-    value_heads = values.reshape(member_rows, realization_number, HEADS, depth)
-    scores = jnp.einsum(
-        "mqhd,mkhd->mhqk", query_heads, key_heads, preferred_element_type=jnp.float32
-    ) / jnp.sqrt(jnp.float32(depth))
-    query_pos = leading_realization + lax.iota(jnp.int32, queries)
-    key_pos = leading_realization - HALF + lax.iota(jnp.int32, realization_number)
-    allowed = (key_pos[None, :] >= query_pos[:, None] - HALF) & (
-        key_pos[None, :] < query_pos[:, None] + HALF
-    )
-    allowed = allowed & (key_pos[None, :] >= 0) & (key_pos[None, :] < total)
-    raised = jnp.where(allowed[None, None], jnp.exp(scores), jnp.float32(0.0))
-    probs = (raised / jnp.sum(raised, axis=-1, keepdims=True)).astype(jnp.bfloat16)
-    mixed = jnp.einsum("mhqk,mkhd->mqhd", probs, value_heads, preferred_element_type=jnp.float32)
-    return mixed.reshape(member_rows, queries, width).astype(jnp.bfloat16)
+    flat = pl.BlockSpec((1, tokens, LANES), lambda m, h: (m, 0, h))
+    pair = pl.BlockSpec((2, 1, tokens, LANES), lambda m, h: (0, m, 0, h))
+    size = members * tokens * 3 * tokens * width
+    half = jax.ShapeDtypeStruct(query.shape, jnp.bfloat16)
+    pairs = [
+        jax.ShapeDtypeStruct(own.shape, kind) for kind in (jnp.bfloat16, jnp.float32, jnp.bfloat16)
+    ]
+    if slope is None:
+        return pl.pallas_call(
+            functools.partial(attend_kernel, depth),
+            grid=(members, width // LANES),
+            out_shape=half,
+            in_specs=[flat, pair, pair, pair],
+            out_specs=flat,
+            compiler_params=pltpu.CompilerParams(vmem_limit_bytes=24 * 2**20),
+            cost_estimate=pl.CostEstimate(
+                flops=4 * size, bytes_accessed=16 * query.size, transcendentals=size // depth
+            ),
+        )(query, below, own, above)
+    return pl.pallas_call(
+        functools.partial(attend_back_kernel, depth),
+        grid=(members, width // LANES),
+        out_shape=[half, *pairs],
+        in_specs=[flat, pair, pair, pair, flat],
+        out_specs=[flat, pair, pair, pair],
+        compiler_params=pltpu.CompilerParams(vmem_limit_bytes=24 * 2**20),
+        cost_estimate=pl.CostEstimate(
+            flops=10 * size, bytes_accessed=36 * query.size, transcendentals=size // depth
+        ),
+    )(query, below, own, above, slope)
 
 
 def split_product(left, right, equation):
@@ -359,14 +439,9 @@
 
     (query, key, value), front_pull = jax.vjp(front, state)
     stacked = jnp.stack([key, value])
-    extended = extended_2(stacked, (("token", 2),), HALF)
-    leading_realization = lax.axis_index("token") * tokens
-    total = tokens * lax.axis_size("token")
-
-    def middle(query_in, extended_in):
-        return attend(query_in, extended_in[0], extended_in[1], leading_realization, total)
-
-    attended, middle_pull = jax.vjp(middle, query, extended)
+    below = from_behind(stacked, "token", 1)
+    above = from_behind(stacked, "token", -1)
+    attended = attention(query, below, stacked, above)
     flat_att = attended.reshape(member_rows * tokens, width)
     update = jnp.dot(flat_att, weight_out, preferred_element_type=jnp.float32).reshape(
         member_rows, tokens, width
@@ -396,14 +471,12 @@
         .astype(jnp.bfloat16)
         .reshape(member_rows, tokens, width)
     )
-    grad_query, grad_extended = middle_pull(grad_attended)
-    lower_rim = grad_extended[:, :, :HALF]
-    upper_rim = grad_extended[:, :, tokens + HALF :]
-    inner = grad_extended[:, :, HALF : tokens + HALF].astype(jnp.float32)
+    grad_query, lower_rim, inner, upper_rim = attention(
+        query, below, stacked, above, grad_attended
+    )
     from_next = from_behind(lower_rim, "token", -1)
     from_prev = from_behind(upper_rim, "token", 1)
-    inner = inner.at[:, :, tokens - HALF :].add(from_next.astype(jnp.float32))
-    inner = inner.at[:, :, :HALF].add(from_prev.astype(jnp.float32))
+    inner = inner + from_next.astype(jnp.float32) + from_prev.astype(jnp.float32)
     (grad_front,) = front_pull(
         (grad_query, inner[0].astype(jnp.bfloat16), inner[1].astype(jnp.bfloat16))
     )

time: 193 us -> 186 us (0.964)
  Pallas kernels: 58.5 us -> 83.4 us
  matrix products: 37 us -> 18.2 us
  other arithmetic: 27.4 us -> 16.2 us
  starting transfers between devices: 18.3 us -> 13 us
  local copies, waits for them, and re-layouts: 29.2 us -> 33.7 us
    pallas_call x0 -> x2, Pallas kernels: none -> 28.1 us  [the longest x1 17 us: attention(): pl.pallas_call(functools.partial(attend_back_kernel, depth), grid=(member...]
    dot_general x6 -> x0, matrix products: 17.7 us -> none  [the longest x3 8.98 us: attend(): jnp.einsum('mqhd,mkhd->mhqk', query_heads, key_heads, preferred_element_t...]
    convert_element_type x1 -> x4, local copies, waits for them, and re-layouts: 2.05 us -> 8.18 us  [project(): normalize_heads(jnp.dot(flat, weight_query, preferred_element_type=jnp.fl...]
    concatenate x1 -> x0, other arithmetic: 5.75 us -> none  [extended_2(): block = jnp.concatenate([low, block, high], axis=dim)]
    ppermute x2 -> x0, starting transfers between devices: 5.3 us -> none  [the longest x1 4.02 us: extended_2(): lax.ppermute(lax.slice_in_dim(block, block.shape[dim] - width, None, axis...]
    reshape x4 -> x0, local copies, waits for them, and re-layouts: 4.93 us -> none  [the longest x1 1.62 us: middle(): extended_in[1]]
    reduce_sum x2, other arithmetic: 0.29 us -> 3.69 us  [normalize_heads(): split * lax.rsqrt(jnp.mean(split * split, axis=-1, keepdims=True) + EPSILON)]
    convert_element_type x2 -> x4, local copies, waits for them, and re-layouts: 3.32 us -> 6.54 us  [project(): normalize_heads(jnp.dot(flat, weight_key, preferred_element_type=jnp.floa...]
  transfers between devices with their start and end apart: 4 -> 4, of which waited for: 0 -> 0; matrix products, arithmetic and copies ran while one was open for 7% -> 13% of each run, Pallas kernels for 30% -> 30%
where the time goes in v3:
time: 186 us
  Pallas kernels  83.4 us (45%)
  local copies, waits for them, and re-layouts  33.7 us (18%)
  matrix products  18.2 us (10%)
  other arithmetic  16.2 us (9%)
  blocking collectives  16.1 us (9%)
  starting transfers between devices  13 us (7%)
  between operations  4.96 us (3%)
    pallas_call x1, Pallas kernels, reduce_gradients(): pl.pallas_call(functools.partial(reduce_kernel, (groups, bits)), out_shap...  55.3 us
    unnamed x73, local copies, waits for them, and re-layouts  17.7 us
    pallas_call x1, Pallas kernels, attention(): pl.pallas_call(functools.partial(attend_back_kernel, depth), grid=(member...  17 us
    all_gather x1, blocking collectives, score_and_slope(): everyone = lax.all_gather(own, 'member', axis=0, tiled=True)  16.1 us
    ppermute x4, starting transfers between devices, from_behind(): return lax.ppermute(block, axis, route)  13 us
    pallas_call x1, Pallas kernels, attention(): pl.pallas_call(functools.partial(attend_kernel, depth), grid=(members, wi...  11.1 us
    convert_element_type x4, local copies, waits for them, and re-layouts, project(): normalize_heads(jnp.dot(flat, weight_query, preferred_element_type=jnp.fl...  8.18 us
    convert_element_type x4, local copies, waits for them, and re-layouts, project(): normalize_heads(jnp.dot(flat, weight_key, preferred_element_type=jnp.floa...  6.54 us
  transfers between devices with their start and end apart: 4, of which 0 were waited for; matrix products, arithmetic and copies ran while one was open for 13% of the time, Pallas kernels for 30%

profile of v3, /device:TPU:0, one launch (start us, length us, event | category | flops | bytes accessed | tf_op | source)
XLA Modules:
  0.0 185.5 jit_solution(13454194523437738982)
XLA Ops:
  0.6 1.6 multiply_reduce_fusion.4
  2.3 4.0 %copy.35 = bf16[1024,1024]{0,1:T(8,128)(2,1)} copy(bf16[1024,1024]{1,0:T(8,128)(2,1)} %param.21) | data formatting | bytes 4194304 | tf_op args[4]
  6.6 2.5 %multiply_reduce_fusion.2 = (f32[256,16]{0,1:T(8,128)S(1)}, f32[256,16,64]{0,2,1:T(8,128)S(1)}) fusion(bf16[256,1024,1]{1,0,2:T(8,128)(2,1)S(1)} %bitcast.93, bf16[16,64,1024]{2,1,0:T(8,128)(2,1)} %bitcast.89), kind=kOutput, calls=%fused_computation.33 | convolution fusion | flops 537391104 | bytes 3686400 | tf_op jit(solution)/shard_map/jvp()/dot_general | solution.py:41
  11.5 2.5 %convolution_convert_fusion.4 = bf16[256,1024]{1,0:T(8,128)(2,1)S(1)} fusion(bf16[256,1024]{1,0:T(8,128)(2,1)} %bitcast.94, bf16[1024,1024]{1,0:T(8,128)(2,1)} %param.22), kind=kOutput, calls=%fused_computation.14 | convolution fusion | flops 537133056 | bytes 3145728 | tf_op jit(solution)/shard_map/jvp()/dot_general | solution.py:44
  15.4 4.1 %collective-permute-start = (bf16[2,2,128,1024]{3,2,1,0:T(8,128)(2,1)S(1)}, bf16[2,2,128,1024]{3,2,1,0:T(8,128)(2,1)}, u32[]{:S(2)}, u32[]{:S(2)}) collective-permute-start(bf16[2,2,128,1024]{3,2,1,0:T(8,128)(2,1)S(1)} %pad_maximum_fusion.own), channel_id=1, source_target_pairs={{0,1},{1,2},{2,3},{3,4},{4,5},{5,6},{6,7},{8,9},{9,10},{10,11},{11... | collective-permute-start | bytes 3145736 | tf_op jit(solution)/shard_map/ppermute | solution.py:21
  19.5 4.0 %copy.34 = bf16[1024,1024]{0,1:T(8,128)(2,1)} copy(bf16[1024,1024]{1,0:T(8,128)(2,1)} %param.20) | data formatting | bytes 4194304 | tf_op args[3]
  23.5 2.5 %multiply_reduce_fusion.3 = (f32[256,16]{0,1:T(8,128)S(1)}, f32[256,16,64]{0,2,1:T(8,128)S(1)}) fusion(bf16[256,1024,1]{1,0,2:T(8,128)(2,1)} %bitcast.95, bf16[16,64,1024]{2,1,0:T(8,128)(2,1)} %bitcast.90), kind=kOutput, calls=%fused_computation.35 | convolution fusion | flops 537391104 | bytes 3686400 | tf_op jit(solution)/shard_map/jvp()/dot_general | solution.py:38
  27.9 2.0 %convert_element_type.124 = bf16[2,128,1024]{1,0,2:T(2,128)(2,1)} reshape(bf16[256,16,64]{0,2,1:T(8,128)(2,1)} %multiply_convert_fusion.1) | data formatting | bytes 1048576 | tf_op jit(solution)/shard_map/jvp()/convert_element_type | solution.py:38
  29.9 2.0 %copy.37.query = bf16[2,128,1024]{2,1,0:T(8,128)(2,1)} copy(bf16[2,128,1024]{1,0,2:T(2,128)(2,1)} %convert_element_type.124) | data formatting | bytes 1048576 | tf_op jit(solution)/shard_map/jvp()/convert_element_type | solution.py:38
  33.4 11.1 %shard_map.156 = bf16[2,128,1024]{2,1,0:T(8,128)(2,1)S(1)} custom-call(bf16[2,128,1024]{2,1,0:T(8,128)(2,1)S(1)} %copy-done.2, bf16[2,2,128,1024]{3,2,1,0:T(8,128)(2,1)} %collective-permute-done.below, bf16[2,2,128,1024]{3,2,1,0:T(8,128)(2,1)S(1)} %pad_maximum_fusion.own, bf16[2,2,128,1024]{3,2,1,0:T(8,128)(2,1)} %collective-permute-done.1.above), custom_call_target="tpu_custom_call" | custom-call | flops 402653184 | bytes 4194304 | tf_op jit(solution)/shard_map/pallas_call | solution.py:140
  45.8 16.1 %all_gather.3 = f32[8,100,128]{2,1,0:T(8,128)S(1)} all-gather(f32[2,100,128]{2,1,0:T(8,128)S(1)} %fusion.11), channel_id=1, replica_groups=mesh['member'=4,'token'=8] {'member'}, dimensions={0}, use_global_device_ids=true | all-gather | bytes 512000 | tf_op jit(solution)/shard_map/all_gather | solution.py:176
  66.0 2.1 %bitcast_convert_fusion = bf16[1024,1024]{1,0:T(8,128)(2,1)} fusion(bf16[2,128,1024]{2,1,0:T(8,128)(2,1)S(1)} %shard_map.156, bf16[2,128,1024]{2,1,0:T(8,128)(2,1)S(1)} %convolution_convert_fusion.5), kind=kOutput, calls=%fused_computation | convolution fusion | flops 537919488 | bytes 3145728 | tf_op jit(solution)/shard_map/dot_general | solution.py:485
  68.8 17.0 %shard_map.158 = (bf16[2,128,1024]{2,1,0:T(8,128)(2,1)S(1)}, bf16[2,2,128,1024]{3,2,1,0:T(8,128)(2,1)}, f32[2,2,128,1024]{3,2,1,0:T(8,128)S(1)}, bf16[2,2,128,1024]{3,2,1,0:T(8,128)(2,1)}) custom-call(bf16[2,128,1024]{2,1,0:T(8,128)(2,1)S(1)} %copy-done.2, bf16[2,2,128,1024]{3,2,1,0:T(8,128)(2,1)} %collective-permute-done.below, ...), custom_call_target="tpu_custom_call" | custom-call | flops 1006632960 | bytes 9437184 | tf_op jit(solution)/shard_map/pallas_call | solution.py:151
  89.2 6.3 %collective-permute-start.3 = (bf16[2,2,128,1024]{3,2,1,0:T(8,128)(2,1)}, bf16[2,2,128,1024]{3,2,1,0:T(8,128)(2,1)}, u32[]{:S(2)}, u32[]{:S(2)}) collective-permute-start(bf16[2,2,128,1024]{3,2,1,0:T(8,128)(2,1)} %get-tuple-element.37), channel_id=1, source_target_pairs={{0,1},{1,2},{2,3},{3,4},{4,5},{5,6},{6,7},{8,9},{9,10},{10,11},{11... | collective-permute-start | bytes 3145736 | tf_op jit(solution)/shard_map/ppermute | solution.py:21
  97.4 1.7 fusion.38
  101.0 1.6 copy-done.1
  102.5 55.3 %shard_map.157 = (f32[128,1024]{1,0:T(8,128)S(1)}, f32[8,16,1024]{2,1,0:T(8,128)S(1)}) custom-call(bf16[4,2,128,1024]{3,2,1,0:T(8,128)(2,1)S(1)} %bitcast.83, f32[4,2,16,1024]{3,2,1,0:T(8,128)S(1)} %bitcast.84), custom_call_target="tpu_custom_call" | custom-call | tf_op jit(solution)/shard_map/pallas_call | solution.py:400
  160.3 3.0 %reshape.400 = f32[256,16,64]{0,2,1:T(8,128)} reshape(f32[2,128,1024]{1,0,2:T(2,128)} %copy.41) | data formatting | bytes 2097152 | tf_op jit(solution)/shard_map/transpose(jvp())/convert_element_type | solution.py:38
  164.2 1.8 multiply_reduce_fusion
  166.5 1.6 fusion.50
  168.1 2.1 %add_convert_fusion = bf16[2,2,128,1024]{3,2,1,0:T(8,128)(2,1)S(1)} fusion(bf16[2,2,128,1024]{3,2,1,0:T(8,128)(2,1)} %collective-permute-done.3, f32[2,2,128,1024]{3,2,1,0:T(8,128)S(1)} %copy-done.4, bf16[2,2,128,1024]{3,2,1,0:T(8,128)(2,1)} %collective-permute-done.2), kind=kLoop, calls=%fused_computation.3 | loop fusion | flops 2621440 | bytes 5242880 | tf_op jit(solution)/shard_map/convert.4
  171.4 2.2 %copy.40 = f32[1,2,128,1024]{2,1,3,0:T(2,128)} copy(f32[1,2,128,1024]{3,2,1,0:T(8,128)} %get-tuple-element.41) | data formatting | bytes 2097152 | tf_op jit(solution)/shard_map/transpose(jvp())/convert_element_type | solution.py:41
  173.6 3.1 %reshape.399 = f32[256,16,64]{0,2,1:T(8,128)} reshape(f32[1,2,128,1024]{2,1,3,0:T(2,128)} %copy.40) | data formatting | bytes 2097152 | tf_op jit(solution)/shard_map/transpose(jvp())/convert_element_type | solution.py:41
  176.7 1.8 multiply_reduce_fusion.1
  (113 shorter events, 28.5 us)
Async XLA Ops:
  0.6 43.9 %copy-start = (bf16[1024,1024]{1,0:T(8,128)(2,1)S(1)}, bf16[1024,1024]{1,0:T(8,128)(2,1)}, u32[]{:S(2)}) copy-start(bf16[1024,1024]{1,0:T(8,128)(2,1)} %param.23) | copy-start | bytes 6291460
  2.3 4.1 %copy-start.14 = (bf16[2,128,1024]{2,1,0:T(8,128)(2,1)S(1)}, bf16[2,128,1024]{2,1,0:T(8,128)(2,1)}, u32[]{:S(2)}) copy-start(bf16[2,128,1024]{2,1,0:T(8,128)(2,1)} %param.18) | copy-start | bytes 1572868
  2.3 4.1 %copy-start.17 = (bf16[2,128,1024]{2,1,0:T(8,128)(2,1)S(1)}, bf16[2,128,1024]{2,1,0:T(8,128)(2,1)}, u32[]{:S(2)}) copy-start(bf16[2,128,1024]{2,1,0:T(8,128)(2,1)} %param.17) | copy-start | bytes 1572868
  2.3 4.1 %copy-start.28 = (f32[1024]{0:T(1024)S(1)}, f32[1024]{0:T(1024)}, u32[]{:S(2)}) copy-start(f32[1024]{0:T(1024)} %param.19) | copy-start | bytes 12292
  6.6 2.6 %copy-start.26 = (bf16[2,128,1024]{2,1,0:T(8,128)(2,1)}, bf16[2,128,1024]{2,1,0:T(8,128)(2,1)S(1)}, u32[]{:S(2)}) copy-start(bf16[2,128,1024]{2,1,0:T(8,128)(2,1)S(1)} %multiply_convert_fusion.2) | copy-start | bytes 1572868
  11.5 2.5 %copy-start.24 = (bf16[1,2,128,1024]{3,2,1,0:T(8,128)(2,1)S(1)}, bf16[1,2,128,1024]{3,2,1,0:T(8,128)(2,1)}, u32[]{:S(2)}) copy-start(bf16[1,2,128,1024]{3,2,1,0:T(8,128)(2,1)} %copy.36) | copy-start | bytes 1572868
  14.1 18.2 %collective-permute-start.1 = (bf16[2,2,128,1024]{3,2,1,0:T(8,128)(2,1)S(1)}, bf16[2,2,128,1024]{3,2,1,0:T(8,128)(2,1)}, u32[]{:S(2)}, u32[]{:S(2)}) collective-permute-start(bf16[2,2,128,1024]{3,2,1,0:T(8,128)(2,1)S(1)} %pad_maximum_fusion.own), channel_id=1, source_target_pairs={{1,0},{2,1},{3,2},{4,3},{5,4},{6,5},{7,6},{9,8},{10,9},{11,10},{12... | collective-permute-start | bytes 3145736 | tf_op jit(solution)/shard_map/ppermute | solution.py:21
  15.4 16.9 %collective-permute-start = (bf16[2,2,128,1024]{3,2,1,0:T(8,128)(2,1)S(1)}, bf16[2,2,128,1024]{3,2,1,0:T(8,128)(2,1)}, u32[]{:S(2)}, u32[]{:S(2)}) collective-permute-start(bf16[2,2,128,1024]{3,2,1,0:T(8,128)(2,1)S(1)} %pad_maximum_fusion.own), channel_id=1, source_target_pairs={{0,1},{1,2},{2,3},{3,4},{4,5},{5,6},{6,7},{8,9},{9,10},{10,11},{11... | collective-permute-start | bytes 3145736 | tf_op jit(solution)/shard_map/ppermute | solution.py:21
  26.0 5.9 %copy-start.29 = (s32[1024]{0:T(1024)S(1)}, s32[1024]{0:T(1024)}, u32[]{:S(2)}) copy-start(s32[1024]{0:T(1024)} %param.29) | copy-start | bytes 12292
  26.0 5.9 %copy-start.30 = (f32[1024]{0:T(1024)S(1)}, f32[1024]{0:T(1024)}, u32[]{:S(2)}) copy-start(f32[1024]{0:T(1024)} %param.27) | copy-start | bytes 12292
  26.0 6.2 %copy-start.31 = (f32[100]{0:T(128)S(1)}, f32[100]{0:T(128)}, u32[]{:S(2)}) copy-start(f32[100]{0:T(128)} %param.28) | copy-start | bytes 1204
  33.4 11.1 %copy-start.15 = (bf16[2,128,1024]{2,1,0:T(8,128)(2,1)S(1)}, bf16[2,128,1024]{2,1,0:T(8,128)(2,1)}, u32[]{:S(2)}) copy-start(bf16[2,128,1024]{2,1,0:T(8,128)(2,1)} %param.18) | copy-start | bytes 1572868
  33.4 11.2 %copy-start.18 = (bf16[2,128,1024]{2,1,0:T(8,128)(2,1)S(1)}, bf16[2,128,1024]{2,1,0:T(8,128)(2,1)}, u32[]{:S(2)}) copy-start(bf16[2,128,1024]{2,1,0:T(8,128)(2,1)} %param.17) | copy-start | bytes 1572868
  45.5 16.9 %copy-start.27 = (f32[100,1024]{1,0:T(8,128)S(1)}, f32[100,1024]{1,0:T(8,128)}, u32[]{:S(2)}) copy-start(f32[100,1024]{1,0:T(8,128)} %param.26) | copy-start | bytes 1228804
  62.0 33.6 %copy-start.7 = (f32[8,100,128]{2,1,0:T(8,128)}, f32[8,100,128]{2,1,0:T(8,128)S(1)}, u32[]{:S(2)}) copy-start(f32[8,100,128]{2,1,0:T(8,128)S(1)} %all_gather.3) | copy-start | bytes 1228804
  66.0 2.8 %copy-start.20 = (bf16[2,128,1024]{2,1,0:T(8,128)(2,1)}, bf16[2,128,1024]{2,1,0:T(8,128)(2,1)S(1)}, u32[]{:S(2)}) copy-start(bf16[2,128,1024]{2,1,0:T(8,128)(2,1)S(1)} %convolution_convert_fusion.5) | copy-start | bytes 1572868
  87.9 80.2 %collective-permute-start.2 = (bf16[2,2,128,1024]{3,2,1,0:T(8,128)(2,1)}, bf16[2,2,128,1024]{3,2,1,0:T(8,128)(2,1)}, u32[]{:S(2)}, u32[]{:S(2)}) collective-permute-start(bf16[2,2,128,1024]{3,2,1,0:T(8,128)(2,1)} %get-tuple-element.36), channel_id=1, source_target_pairs={{1,0},{2,1},{3,2},{4,3},{5,4},{6,5},{7,6},{9,8},{10,9},{11,10},{12... | collective-permute-start | bytes 3145736 | tf_op jit(solution)/shard_map/ppermute | solution.py:21
  89.2 78.9 %collective-permute-start.3 = (bf16[2,2,128,1024]{3,2,1,0:T(8,128)(2,1)}, bf16[2,2,128,1024]{3,2,1,0:T(8,128)(2,1)}, u32[]{:S(2)}, u32[]{:S(2)}) collective-permute-start(bf16[2,2,128,1024]{3,2,1,0:T(8,128)(2,1)} %get-tuple-element.37), channel_id=1, source_target_pairs={{0,1},{1,2},{2,3},{3,4},{4,5},{5,6},{6,7},{8,9},{9,10},{10,11},{11... | collective-permute-start | bytes 3145736 | tf_op jit(solution)/shard_map/ppermute | solution.py:21
  99.8 59.3 %copy-start.6 = (bf16[2,128,1024]{2,1,0:T(8,128)(2,1)S(1)}, bf16[2,128,1024]{2,1,0:T(8,128)(2,1)}, u32[]{:S(2)}) copy-start(bf16[2,128,1024]{2,1,0:T(8,128)(2,1)} %copy-done.5) | copy-start | bytes 1572868
  163.3 2.7 %copy-start.11 = (f32[256,16,64]{0,2,1:T(8,128)S(1)}, f32[256,16,64]{0,2,1:T(8,128)}, u32[]{:S(2)}) copy-start(f32[256,16,64]{0,2,1:T(8,128)} %copy-done.10) | copy-start | bytes 3145732
  163.3 2.7 %copy-start.12 = (f32[256,16,64]{0,2,1:T(8,128)S(1)}, f32[256,16,64]{0,2,1:T(8,128)}, u32[]{:S(2)}) copy-start(f32[256,16,64]{0,2,1:T(8,128)} %reshape.400) | copy-start | bytes 3145732
  164.1 2.4 %copy-start.22 = (bf16[1024,1024]{1,0:T(8,128)(2,1)S(1)}, bf16[1024,1024]{1,0:T(8,128)(2,1)}, u32[]{:S(2)}) copy-start(bf16[1024,1024]{1,0:T(8,128)(2,1)} %param.20) | copy-start | bytes 6291460
  176.7 2.2 %copy-start.13 = (f32[256,16,64]{0,2,1:T(8,128)S(1)}, f32[256,16,64]{0,2,1:T(8,128)}, u32[]{:S(2)}) copy-start(f32[256,16,64]{0,2,1:T(8,128)} %reshape.399) | copy-start | bytes 3145732
  176.7 2.9 %copy-start.23 = (bf16[1024,1024]{1,0:T(8,128)(2,1)S(1)}, bf16[1024,1024]{1,0:T(8,128)(2,1)}, u32[]{:S(2)}) copy-start(bf16[1024,1024]{1,0:T(8,128)(2,1)} %param.21) | copy-start | bytes 6291460
  (15 other events, 19.5 us)

commit v4 on v3

--- a/solution.py
+++ b/solution.py
@@ -21,11 +21,38 @@
     return lax.ppermute(block, axis, route)
 
 
+def head_places(width):
+    feature = lax.broadcasted_iota(jnp.int32, (width, HEADS), 0) // (width // HEADS)
+    return (feature == lax.broadcasted_iota(jnp.int32, (width, HEADS), 1)).astype(jnp.bfloat16)
+
+
+def head_mean(flat):
+    width = flat.shape[1]
+    return split_product(flat, head_places(width), "rc,ch->rh") * (HEADS / width)
+
+
+def over_heads(each, width):
+    return split_product(each, head_places(width), "rh,ch->rc")
+
+
+@jax.custom_vjp
 def normalize_heads(flat):
-    rows, width = flat.shape
-    split = flat.reshape(rows, HEADS, width // HEADS)
-    split = split * lax.rsqrt(jnp.mean(split * split, axis=-1, keepdims=True) + EPSILON)
-    return split.reshape(rows, width)
+    return normalize_heads_forward(flat)[0]
+
+
+def normalize_heads_forward(flat):
+    inverse = lax.rsqrt(head_mean(flat * flat) + EPSILON)
+    return flat * over_heads(inverse, flat.shape[1]), (flat, inverse)
+
+
+def normalize_heads_back(saved, slope):
+    flat, inverse = saved
+    width = flat.shape[1]
+    pulled = head_mean(slope * flat) * inverse * inverse * inverse
+    return (slope * over_heads(inverse, width) - flat * over_heads(pulled, width),)
+
+
+normalize_heads.defvjp(normalize_heads_forward, normalize_heads_back)
 
 
 def project(state_in, member_noise, norm_gain, weight_query, weight_key, weight_value):
@@ -168,12 +195,55 @@
     return first + jnp.einsum(equation, low, right, preferred_element_type=jnp.float32)
 
 
+def gather_kernel(groups, own, out, slots, sends, recvs):
+    here = lax.axis_index("member")
+    barrier = pltpu.get_barrier_semaphore()
+    for ahead in range(1, groups):
+        pl.semaphore_signal(
+            barrier, inc=1, device_id={"member": lax.rem(here + ahead, groups)},
+            device_id_type=pl.DeviceIdType.MESH,
+        )
+    pl.semaphore_wait(barrier, groups - 1)
+    copies = []
+    for ahead in range(1, groups):
+        copy = pltpu.make_async_remote_copy(
+            src_ref=own, dst_ref=slots.at[here],
+            send_sem=sends.at[ahead - 1], recv_sem=recvs.at[ahead - 1],
+            device_id={"member": lax.rem(here + ahead, groups)},
+            device_id_type=pl.DeviceIdType.MESH,
+        )
+        copy.start()
+        copies.append(copy)
+    slots[here] = own[...]
+    for copy in copies:
+        copy.wait()
+    out[...] = slots[...]
+
+
+def gather_members(own):
+    groups = lax.axis_size("member")
+    shape = (groups, *own.shape)
+    gathered = pl.pallas_call(
+        functools.partial(gather_kernel, groups),
+        out_shape=jax.ShapeDtypeStruct(shape, own.dtype),
+        in_specs=[pl.BlockSpec(memory_space=pltpu.VMEM)],
+        out_specs=pl.BlockSpec(memory_space=pltpu.VMEM),
+        scratch_shapes=[
+            pltpu.VMEM(shape, own.dtype),
+            pltpu.SemaphoreType.DMA((groups - 1,)),
+            pltpu.SemaphoreType.DMA((groups - 1,)),
+        ],
+        compiler_params=pltpu.CompilerParams(collective_id=1, has_side_effects=True),
+    )(own)
+    return gathered.reshape(groups * own.shape[0], *own.shape[1:])
+
+
 def score_and_slope(own, observed, surface_extent, quantity, point_map):
     member_rows, _, tokens = own.shape
     onehot = point_map[:, None] == lax.iota(jnp.int32, tokens)[None, :]
     token_area = jnp.sum(jnp.where(onehot, surface_extent[:, None], 0.0), axis=0)
     onehot = onehot.astype(jnp.bfloat16)
-    everyone = lax.all_gather(own, "member", axis=0, tiled=True)
+    everyone = gather_members(own)
     count = everyone.shape[0]
     diff = split_product(own, onehot, "mvt,pt->mvp") - observed[None]
     inverse = lax.rsqrt(diff * diff + SMOOTH)

time: 186 us -> 190 us (1.022)
  the two profiles are of different devices: /device:TPU:0 before, /device:TPU:6 now
where the time goes in v4:
time: 190 us; the launch traced here: 189 us
  Pallas kernels  84.3 us (44%)
  matrix products  44 us (23%)
  waiting for transfers between devices  25.2 us (13%)
  other arithmetic  12.3 us (6%)
  starting transfers between devices  11.2 us (6%)
  local copies, waits for them, and re-layouts  7.23 us (4%)
  between operations  4.99 us (3%)
    pallas_call x1, Pallas kernels, reduce_gradients(): pl.pallas_call(functools.partial(reduce_kernel, (groups, bits)), out_shap...  45.5 us
    ppermute x4, waiting for transfers between devices, from_behind(): return lax.ppermute(block, axis, route)  25.2 us
    pallas_call x1, Pallas kernels, attention(): pl.pallas_call(functools.partial(attend_back_kernel, depth), grid=(member...  17 us
    ppermute x4, starting transfers between devices, from_behind(): return lax.ppermute(block, axis, route)  11.2 us
    pallas_call x1, Pallas kernels, attention(): pl.pallas_call(functools.partial(attend_kernel, depth), grid=(members, wi...  11.1 us
    pallas_call x1, Pallas kernels, gather_members(): pl.pallas_call(functools.partial(gather_kernel, groups), out_shape=jax.Sh...  10.6 us
    dot_general x6, matrix products, split_product(): jnp.einsum(equation, low, right, preferred_element_type=jnp.float32)  8.71 us
    dot_general x2, matrix products, project(): jnp.dot(flat, weight_query, preferred_element_type=jnp.float32)  7.04 us
  transfers between devices with their start and end apart: 4, of which 2 were waited for; matrix products, arithmetic and copies ran while one was open for 9% of the time, Pallas kernels for 0%

profile of v4, /device:TPU:6, one launch (start us, length us, event | category | flops | bytes accessed | tf_op | source)
XLA Modules:
  0.0 189.2 jit_solution(4627443881194995298)
XLA Ops:
  0.7 1.6 multiply_reduce_fusion
  9.3 2.1 %multiply_convert_fusion = (bf16[256,1024]{1,0:T(8,128)(2,1)S(1)}, f32[256,1024]{1,0:T(8,128)}) fusion(f32[256,1024]{1,0:T(8,128)S(1)} %fusion.148, f32[256,1024]{1,0:T(8,128)S(1)} %fusion.56, s32[1024]{0:T(1024)S(1)} %get-tuple-element.48, s32[1024]{0:T(1024)S(1)} %get-tuple-element.49, pred[1024]{0:T(1024)(128)(4,1)S(1)} %fusion.142, ...), kind=kOutput, calls=%fused_computation.60 | convolution fusion | flops 9224192 | bytes 3695616 | tf_op jit(solution)/shard_map/jvp(rh,ch->rc)/dot_general | solution.py:195
  11.4 1.9 %collective-permute-start.1 = (bf16[2,2,128,1024]{3,2,1,0:T(8,128)(2,1)S(1)}, bf16[2,2,128,1024]{3,2,1,0:T(8,128)(2,1)}, u32[]{:S(2)}, u32[]{:S(2)}) collective-permute-start(bf16[2,2,128,1024]{3,2,1,0:T(8,128)(2,1)S(1)} %pad_maximum_fusion.own), channel_id=1, source_target_pairs={{1,0},{2,1},{3,2},{4,3},{5,4},{6,5},{7,6},{9,8},{10,9},{11,10},{12... | collective-permute-start | bytes 3145736 | tf_op jit(solution)/shard_map/ppermute | solution.py:21
  13.3 3.6 %collective-permute-start = (bf16[2,2,128,1024]{3,2,1,0:T(8,128)(2,1)S(1)}, bf16[2,2,128,1024]{3,2,1,0:T(8,128)(2,1)}, u32[]{:S(2)}, u32[]{:S(2)}) collective-permute-start(bf16[2,2,128,1024]{3,2,1,0:T(8,128)(2,1)S(1)} %pad_maximum_fusion.own), channel_id=1, source_target_pairs={{0,1},{1,2},{2,3},{3,4},{4,5},{5,6},{6,7},{8,9},{9,10},{10,11},{11... | collective-permute-start | bytes 3145736 | tf_op jit(solution)/shard_map/ppermute | solution.py:21
  17.1 2.5 %fusion.147 = f32[256,1024]{1,0:T(8,128)S(1)} fusion(bf16[256,1024]{1,0:T(8,128)(2,1)} %bitcast.89, bf16[1024,1024]{1,0:T(8,128)(2,1)} %param.20), kind=kOutput, calls=%fused_computation.222 | convolution fusion | flops 536870912 | bytes 3670016 | tf_op jit(solution)/shard_map/jvp()/dot_general | solution.py:65
  23.8 2.1 %multiply_convert_fusion.1 = (bf16[256,1024]{1,0:T(8,128)(2,1)S(1)}, f32[256,1024]{1,0:T(8,128)}) fusion(f32[256,1024]{1,0:T(8,128)S(1)} %fusion.147, f32[256,1024]{1,0:T(8,128)S(1)} %fusion.57, s32[1024]{0:T(1024)S(1)} %get-tuple-element.48, s32[1024]{0:T(1024)S(1)} %get-tuple-element.49, pred[1024]{0:T(1024)(128)(4,1)S(1)} %fusion.142, ...), kind=kOutput, calls=%fused_computation.62 | convolution fusion | flops 9224192 | bytes 3695616 | tf_op jit(solution)/shard_map/jvp(rh,ch->rc)/dot_general | solution.py:195
  25.9 12.9 %collective-permute-done.below = bf16[2,2,128,1024]{3,2,1,0:T(8,128)(2,1)} collective-permute-done((bf16[2,2,128,1024]{3,2,1,0:T(8,128)(2,1)S(1)}, bf16[2,2,128,1024]{3,2,1,0:T(8,128)(2,1)}, u32[]{:S(2)}, u32[]{:S(2)}) %collective-permute-start) | collective-permute-done | bytes 1048608 | tf_op jit(solution)/shard_map/ppermute | solution.py:21
  38.8 11.1 %shard_map.156 = bf16[2,128,1024]{2,1,0:T(8,128)(2,1)S(1)} custom-call(bf16[2,128,1024]{2,1,0:T(8,128)(2,1)S(1)} %bitcast.74, bf16[2,2,128,1024]{3,2,1,0:T(8,128)(2,1)} %collective-permute-done.below, bf16[2,2,128,1024]{3,2,1,0:T(8,128)(2,1)S(1)} %pad_maximum_fusion.own, bf16[2,2,128,1024]{3,2,1,0:T(8,128)(2,1)} %collective-permute-done.1.above), custom_call_target="tpu_custom_call" | custom-call | flops 402653184 | bytes 4194304 | tf_op jit(solution)/shard_map/pallas_call | solution.py:167
  52.5 10.6 %shard_map.157 = f32[4,2,100,128]{3,2,1,0:T(8,128)} custom-call(f32[2,100,128]{2,1,0:T(8,128)} %fusion.13.own), custom_call_target="tpu_custom_call" | custom-call | tf_op jit(solution)/shard_map/pallas_call | solution.py:226
  64.5 2.4 %multiply_reduce_fusion.1 = (f32[]{:T(128)}, f32[2,100,1024]{2,1,0:T(8,128)S(1)}) fusion(f32[100,1024]{1,0:T(8,128)} %multiply_multiply_fusion, f32[100,1024]{1,0:T(8,128)} %param.26, f32[2,100,1024]{2,1,0:T(8,128)S(1)} %fusion.52, s32[1024]{0:T(1024)S(1)} %copy-done.32, f32[2,100,128]{2,1,0:T(8,128)} %fusion.13.own), kind=kOutput, calls=%fused_computation.69 | convolution fusion | flops 54095872 | bytes 2564100 | tf_op jit(solution)/shard_map/mvt,pt->mvp/dot_general | solution.py:195
  69.5 2.1 %bitcast_convert_fusion = bf16[1024,1024]{1,0:T(8,128)(2,1)} fusion(bf16[2,128,1024]{2,1,0:T(8,128)(2,1)S(1)} %copy-done.7, bf16[2,128,1024]{2,1,0:T(8,128)(2,1)S(1)} %convolution_convert_fusion.5), kind=kOutput, calls=%fused_computation | convolution fusion | flops 537919488 | bytes 3145728 | tf_op jit(solution)/shard_map/dot_general | solution.py:555
  73.6 1.7 fusion.124
  77.1 1.6 copy-done.1
  78.7 45.5 %shard_map.158 = (f32[128,1024]{1,0:T(8,128)S(1)}, f32[8,16,1024]{2,1,0:T(8,128)S(1)}) custom-call(bf16[4,2,128,1024]{3,2,1,0:T(8,128)(2,1)S(1)} %bitcast.70, f32[4,2,16,1024]{3,2,1,0:T(8,128)S(1)} %bitcast.76), custom_call_target="tpu_custom_call" | custom-call | tf_op jit(solution)/shard_map/pallas_call | solution.py:470
  126.3 17.0 %shard_map.159 = (bf16[2,128,1024]{2,1,0:T(8,128)(2,1)S(1)}, bf16[2,2,128,1024]{3,2,1,0:T(8,128)(2,1)}, f32[2,2,128,1024]{3,2,1,0:T(8,128)S(1)}, bf16[2,2,128,1024]{3,2,1,0:T(8,128)(2,1)}) custom-call(bf16[2,128,1024]{2,1,0:T(8,128)(2,1)S(1)} %bitcast.75, bf16[2,2,128,1024]{3,2,1,0:T(8,128)(2,1)} %collective-permute-done.below, ...), custom_call_target="tpu_custom_call" | custom-call | flops 1006632960 | bytes 9437184 | tf_op jit(solution)/shard_map/pallas_call | solution.py:178
  143.4 1.9 %collective-permute-start.2 = (bf16[2,2,128,1024]{3,2,1,0:T(8,128)(2,1)}, bf16[2,2,128,1024]{3,2,1,0:T(8,128)(2,1)}, u32[]{:S(2)}, u32[]{:S(2)}) collective-permute-start(bf16[2,2,128,1024]{3,2,1,0:T(8,128)(2,1)} %get-tuple-element.36), channel_id=1, source_target_pairs={{1,0},{2,1},{3,2},{4,3},{5,4},{6,5},{7,6},{9,8},{10,9},{11,10},{12... | collective-permute-start | bytes 3145736 | tf_op jit(solution)/shard_map/ppermute | solution.py:21
  145.3 3.7 %collective-permute-start.3 = (bf16[2,2,128,1024]{3,2,1,0:T(8,128)(2,1)}, bf16[2,2,128,1024]{3,2,1,0:T(8,128)(2,1)}, u32[]{:S(2)}, u32[]{:S(2)}) collective-permute-start(bf16[2,2,128,1024]{3,2,1,0:T(8,128)(2,1)} %get-tuple-element.37), channel_id=1, source_target_pairs={{0,1},{1,2},{2,3},{3,4},{4,5},{5,6},{6,7},{8,9},{9,10},{10,11},{11... | collective-permute-start | bytes 3145736 | tf_op jit(solution)/shard_map/ppermute | solution.py:21
  151.4 2.1 %fusion.54 = f32[256,1024]{1,0:T(8,128)} fusion(s32[1024]{0:T(1024)S(1)} %get-tuple-element.48, s32[1024]{0:T(1024)S(1)} %get-tuple-element.49, pred[1024]{0:T(1024)(128)(4,1)S(1)} %fusion.142, f32[256,16]{0,1:T(8,128)S(1)} %fusion.17), kind=kOutput, calls=%fused_computation.89 | convolution fusion | flops 8425472 | bytes 1074176 | tf_op jit(solution)/shard_map/transpose(jvp(rh,ch->rc))/dot_general | solution.py:65
  153.5 4.6 %convolution_convert_fusion = bf16[256,1024]{1,0:T(8,128)(2,1)} fusion(bf16[1024,1024]{1,0:T(8,128)(2,1)} %param.20, f32[256,1024]{1,0:T(8,128)} %get-tuple-element.43, bf16[256,1024]{1,0:T(8,128)(2,1)} %bitcast.73, f32[256,1024]{1,0:T(8,128)S(1)} %copy-done.14, f32[256,1024]{1,0:T(8,128)} %fusion.54, s32[1024]{0:T(1024)S(1)} %get-tuple-element.48, ...), kind=kOutput, calls=%fused_computation.18 | convolution fusion | flops 546881536 | bytes 6317056 | tf_op jit(solution)/shard_map/transpose(jvp())/dot_general | solution.py:65
  158.1 12.3 %collective-permute-done.3 = bf16[2,2,128,1024]{3,2,1,0:T(8,128)(2,1)} collective-permute-done((bf16[2,2,128,1024]{3,2,1,0:T(8,128)(2,1)}, bf16[2,2,128,1024]{3,2,1,0:T(8,128)(2,1)}, u32[]{:S(2)}, u32[]{:S(2)}) %collective-permute-start.3) | collective-permute-done | bytes 1048608 | tf_op jit(solution)/shard_map/ppermute | solution.py:21
  170.3 2.7 %add_convert_fusion = bf16[2,2,128,1024]{3,2,1,0:T(8,128)(2,1)S(1)} fusion(bf16[2,2,128,1024]{3,2,1,0:T(8,128)(2,1)} %collective-permute-done.3, f32[2,2,128,1024]{3,2,1,0:T(8,128)} %copy-done.5, bf16[2,2,128,1024]{3,2,1,0:T(8,128)(2,1)} %collective-permute-done.2), kind=kLoop, calls=%fused_computation.3 | loop fusion | flops 2621440 | bytes 5242880 | tf_op jit(solution)/shard_map/convert.4
  176.2 2.1 %fusion.55 = f32[256,1024]{1,0:T(8,128)} fusion(s32[1024]{0:T(1024)S(1)} %get-tuple-element.48, s32[1024]{0:T(1024)S(1)} %get-tuple-element.49, pred[1024]{0:T(1024)(128)(4,1)S(1)} %fusion.142, f32[256,16]{0,1:T(8,128)S(1)} %fusion.21), kind=kOutput, calls=%fused_computation.90 | convolution fusion | flops 8425472 | bytes 1074176 | tf_op jit(solution)/shard_map/transpose(jvp(rh,ch->rc))/dot_general | solution.py:68
  178.3 4.5 %convolution_convert_fusion.1 = bf16[256,1024]{1,0:T(8,128)(2,1)} fusion(bf16[1024,1024]{1,0:T(8,128)(2,1)} %param.21, f32[256,1024]{1,0:T(8,128)} %get-tuple-element.45, bf16[256,1024]{1,0:T(8,128)(2,1)} %bitcast.86, f32[256,1024]{1,0:T(8,128)S(1)} %copy-done.11, f32[256,1024]{1,0:T(8,128)} %fusion.55, s32[1024]{0:T(1024)S(1)} %get-tuple-element.48, ...), kind=kOutput, calls=%fused_computation.19 | convolution fusion | flops 546881536 | bytes 6317056 | tf_op jit(solution)/shard_map/transpose(jvp())/dot_general | solution.py:68
  182.8 2.8 %fusion.12 = bf16[256,1024]{1,0:T(8,128)(2,1)S(1)} fusion(bf16[256,1024]{1,0:T(8,128)(2,1)} %convolution_convert_fusion, bf16[256,1024]{1,0:T(8,128)(2,1)} %convolution_convert_fusion.1, bf16[256,1024]{1,0:T(8,128)(2,1)} %bitcast.93, bf16[1024,1024]{1,0:T(8,128)(2,1)} %param.22), kind=kOutput, calls=%fused_computation.26 | convolution fusion | flops 537657344 | bytes 4194304 | tf_op jit(solution)/shard_map/transpose(jvp())/dot_general | solution.py:71
  (113 shorter events, 28.8 us)
Async XLA Ops:
  0.6 49.3 %copy-start = (bf16[1024,1024]{1,0:T(8,128)(2,1)S(1)}, bf16[1024,1024]{1,0:T(8,128)(2,1)}, u32[]{:S(2)}) copy-start(bf16[1024,1024]{1,0:T(8,128)(2,1)} %param.23) | copy-start | bytes 6291460
  0.6 3.1 %copy-start.36 = (bf16[1024,1024]{1,0:T(8,128)(2,1)S(1)}, bf16[1024,1024]{1,0:T(8,128)(2,1)}, u32[]{:S(2)}) copy-start(bf16[1024,1024]{1,0:T(8,128)(2,1)} %param.22) | copy-start | bytes 6291460
  6.2 5.1 %copy-start.10 = (f32[256,1024]{1,0:T(8,128)}, f32[256,1024]{1,0:T(8,128)S(1)}, u32[]{:S(2)}) copy-start(f32[256,1024]{1,0:T(8,128)S(1)} %fusion.148) | copy-start | bytes 3145732
  11.4 14.5 %collective-permute-start.1 = (bf16[2,2,128,1024]{3,2,1,0:T(8,128)(2,1)S(1)}, bf16[2,2,128,1024]{3,2,1,0:T(8,128)(2,1)}, u32[]{:S(2)}, u32[]{:S(2)}) collective-permute-start(bf16[2,2,128,1024]{3,2,1,0:T(8,128)(2,1)S(1)} %pad_maximum_fusion.own), channel_id=1, source_target_pairs={{1,0},{2,1},{3,2},{4,3},{5,4},{6,5},{7,6},{9,8},{10,9},{11,10},{12... | collective-permute-start | bytes 3145736 | tf_op jit(solution)/shard_map/ppermute | solution.py:21
  13.3 25.5 %collective-permute-start = (bf16[2,2,128,1024]{3,2,1,0:T(8,128)(2,1)S(1)}, bf16[2,2,128,1024]{3,2,1,0:T(8,128)(2,1)}, u32[]{:S(2)}, u32[]{:S(2)}) collective-permute-start(bf16[2,2,128,1024]{3,2,1,0:T(8,128)(2,1)S(1)} %pad_maximum_fusion.own), channel_id=1, source_target_pairs={{0,1},{1,2},{2,3},{3,4},{4,5},{5,6},{6,7},{8,9},{9,10},{10,11},{11... | collective-permute-start | bytes 3145736 | tf_op jit(solution)/shard_map/ppermute | solution.py:21
  17.1 3.4 %copy-start.32 = (s32[1024]{0:T(1024)S(1)}, s32[1024]{0:T(1024)}, u32[]{:S(2)}) copy-start(s32[1024]{0:T(1024)} %param.29) | copy-start | bytes 12292
  17.1 3.4 %copy-start.33 = (f32[1024]{0:T(1024)S(1)}, f32[1024]{0:T(1024)}, u32[]{:S(2)}) copy-start(f32[1024]{0:T(1024)} %param.27) | copy-start | bytes 12292
  17.1 3.7 %copy-start.34 = (f32[100]{0:T(128)S(1)}, f32[100]{0:T(128)}, u32[]{:S(2)}) copy-start(f32[100]{0:T(128)} %param.28) | copy-start | bytes 1204
  19.6 6.3 %copy-start.12 = (f32[256,1024]{1,0:T(8,128)}, f32[256,1024]{1,0:T(8,128)S(1)}, u32[]{:S(2)}) copy-start(f32[256,1024]{1,0:T(8,128)S(1)} %fusion.147) | copy-start | bytes 3145732
  25.9 24.1 %copy-start.3 = (bf16[256,1024]{1,0:T(8,128)(2,1)}, bf16[256,1024]{1,0:T(8,128)(2,1)S(1)}, u32[]{:S(2)}) copy-start(bf16[256,1024]{1,0:T(8,128)(2,1)S(1)} %get-tuple-element.42) | copy-start | bytes 1572868
  38.8 11.2 %copy-start.17 = (bf16[2,128,1024]{2,1,0:T(8,128)(2,1)S(1)}, bf16[2,128,1024]{2,1,0:T(8,128)(2,1)}, u32[]{:S(2)}) copy-start(bf16[2,128,1024]{2,1,0:T(8,128)(2,1)} %param.18) | copy-start | bytes 1572868
  38.8 11.2 %copy-start.19 = (bf16[2,128,1024]{2,1,0:T(8,128)(2,1)S(1)}, bf16[2,128,1024]{2,1,0:T(8,128)(2,1)}, u32[]{:S(2)}) copy-start(bf16[2,128,1024]{2,1,0:T(8,128)(2,1)} %param.17) | copy-start | bytes 1572868
  63.2 3.8 %copy-start.29 = (f32[100,1024]{1,0:T(8,128)S(1)}, f32[100,1024]{1,0:T(8,128)}, u32[]{:S(2)}) copy-start(f32[100,1024]{1,0:T(8,128)} %multiply_multiply_fusion) | copy-start | bytes 1228804
  76.0 49.6 %copy-start.24 = (bf16[2,128,1024]{2,1,0:T(8,128)(2,1)S(1)}, bf16[2,128,1024]{2,1,0:T(8,128)(2,1)}, u32[]{:S(2)}) copy-start(bf16[2,128,1024]{2,1,0:T(8,128)(2,1)} %copy-done.23) | copy-start | bytes 1572868
  126.3 23.3 %copy-start.13 = (f32[256,1024]{1,0:T(8,128)S(1)}, f32[256,1024]{1,0:T(8,128)}, u32[]{:S(2)}) copy-start(f32[256,1024]{1,0:T(8,128)} %copy-done.12) | copy-start | bytes 3145732
  143.4 10.1 %copy-start.2 = (bf16[2,128,1024]{2,1,0:T(8,128)(2,1)}, bf16[2,128,1024]{2,1,0:T(8,128)(2,1)S(1)}, u32[]{:S(2)}) copy-start(bf16[2,128,1024]{2,1,0:T(8,128)(2,1)S(1)} %get-tuple-element.38) | copy-start | bytes 1572868
  143.4 10.1 %copy-start.5 = (f32[2,2,128,1024]{3,2,1,0:T(8,128)}, f32[2,2,128,1024]{3,2,1,0:T(8,128)S(1)}, u32[]{:S(2)}) copy-start(f32[2,2,128,1024]{3,2,1,0:T(8,128)S(1)} %get-tuple-element.35) | copy-start | bytes 6291460
  143.4 14.7 %collective-permute-start.2 = (bf16[2,2,128,1024]{3,2,1,0:T(8,128)(2,1)}, bf16[2,2,128,1024]{3,2,1,0:T(8,128)(2,1)}, u32[]{:S(2)}, u32[]{:S(2)}) collective-permute-start(bf16[2,2,128,1024]{3,2,1,0:T(8,128)(2,1)} %get-tuple-element.36), channel_id=1, source_target_pairs={{1,0},{2,1},{3,2},{4,3},{5,4},{6,5},{7,6},{9,8},{10,9},{11,10},{12... | collective-permute-start | bytes 3145736 | tf_op jit(solution)/shard_map/ppermute | solution.py:21
  145.3 25.0 %collective-permute-start.3 = (bf16[2,2,128,1024]{3,2,1,0:T(8,128)(2,1)}, bf16[2,2,128,1024]{3,2,1,0:T(8,128)(2,1)}, u32[]{:S(2)}, u32[]{:S(2)}) collective-permute-start(bf16[2,2,128,1024]{3,2,1,0:T(8,128)(2,1)} %get-tuple-element.37), channel_id=1, source_target_pairs={{0,1},{1,2},{2,3},{3,4},{4,5},{5,6},{6,7},{8,9},{9,10},{10,11},{11... | collective-permute-start | bytes 3145736 | tf_op jit(solution)/shard_map/ppermute | solution.py:21
  149.7 3.9 %copy-start.14 = (f32[256,1024]{1,0:T(8,128)S(1)}, f32[256,1024]{1,0:T(8,128)}, u32[]{:S(2)}) copy-start(f32[256,1024]{1,0:T(8,128)} %copy-done.12) | copy-start | bytes 3145732
  173.9 4.4 %copy-start.21 = (bf16[1,2,128,1024]{3,2,1,0:T(8,128)(2,1)}, bf16[1,2,128,1024]{3,2,1,0:T(8,128)(2,1)S(1)}, u32[]{:S(2)}) copy-start(bf16[1,2,128,1024]{3,2,1,0:T(8,128)(2,1)S(1)} %get-tuple-element.41) | copy-start | bytes 1572868
  182.8 2.9 %copy-start.20 = (bf16[2,128,1024]{2,1,0:T(8,128)(2,1)S(1)}, bf16[2,128,1024]{2,1,0:T(8,128)(2,1)}, u32[]{:S(2)}) copy-start(bf16[2,128,1024]{2,1,0:T(8,128)(2,1)} %param.17) | copy-start | bytes 1572868
  182.8 2.9 %copy-start.31 = (f32[1024]{0:T(1024)S(1)}, f32[1024]{0:T(1024)}, u32[]{:S(2)}) copy-start(f32[1024]{0:T(1024)} %param.19) | copy-start | bytes 12292
  182.8 3.2 %copy-start.25 = (bf16[2,128,1024]{2,1,0:T(8,128)(2,1)S(1)}, bf16[2,128,1024]{2,1,0:T(8,128)(2,1)}, u32[]{:S(2)}) copy-start(bf16[2,128,1024]{2,1,0:T(8,128)(2,1)} %copy-done.23) | copy-start | bytes 1572868
  (17 other events, 28.3 us)

commit v5 on v4

--- a/solution.py
+++ b/solution.py
@@ -479,6 +479,9 @@
         compiler_params=pltpu.CompilerParams(
             collective_id=0, has_side_effects=True, vmem_limit_bytes=40 * 2**20
         ),
+        cost_estimate=pl.CostEstimate(
+            flops=4 * 10**10, bytes_accessed=4 * product.size, transcendentals=0
+        ),
     )(
         product.reshape(count // 2, 2, rows, width),
         padded.reshape(chunks // 2, 2, deep, width),
@@ -547,19 +550,22 @@
     from_next = from_behind(lower_rim, "token", -1)
     from_prev = from_behind(upper_rim, "token", 1)
     inner = inner + from_next.astype(jnp.float32) + from_prev.astype(jnp.float32)
-    (grad_front,) = front_pull(
-        (grad_query, inner[0].astype(jnp.bfloat16), inner[1].astype(jnp.bfloat16))
-    )
-    grad_members = (grad_front + carried_slope.astype(jnp.float32)).astype(jnp.bfloat16)
     contract = (((0,), (0,)), ((), ()))
     product = lax.dot_general(flat_att, flat_grad, contract, preferred_element_type=jnp.float32)
     variables = decoder_piece.shape[0]
+    product, decoder_piece, grad_query = lax.optimization_barrier(
+        (product, decoder_piece, grad_query)
+    )
     decoder_piece = jnp.concatenate([decoder_piece, jnp.full((1, width), share)])
     grad_out, decoder_sum = reduce_gradients(product.astype(jnp.bfloat16), decoder_piece)
     grad_decoder = decoder_sum[:variables]
     mean_scoring = decoder_sum[variables, 0] / (
         observations.shape[0] * observations.shape[1] * lax.axis_size("token")
     )
+    (grad_front,) = front_pull(
+        (grad_query, inner[0].astype(jnp.bfloat16), inner[1].astype(jnp.bfloat16))
+    )
+    grad_members = (grad_front + carried_slope.astype(jnp.float32)).astype(jnp.bfloat16)
     return (mean_scoring, grad_members, grad_out, grad_decoder)
 
 

time: 190 us -> 192 us (1.011)
  local copies, waits for them, and re-layouts: 7.23 us -> 9.57 us
    unnamed x75 -> x67, local copies, waits for them, and re-layouts: 5.03 us -> 7.38 us
where the time goes in v5:
time: 192 us
  Pallas kernels  84.2 us (44%)
  matrix products  44.3 us (23%)
  waiting for transfers between devices  25.3 us (13%)
  other arithmetic  12.3 us (6%)
  starting transfers between devices  10.9 us (6%)
  local copies, waits for them, and re-layouts  9.57 us (5%)
  between operations  4.99 us (3%)
    pallas_call x1, Pallas kernels, reduce_gradients(): pl.pallas_call(functools.partial(reduce_kernel, (groups, bits)), out_shap...  45.5 us
    ppermute x4, waiting for transfers between devices, from_behind(): return lax.ppermute(block, axis, route)  25.3 us
    pallas_call x1, Pallas kernels, attention(): pl.pallas_call(functools.partial(attend_back_kernel, depth), grid=(member...  16.9 us
    pallas_call x1, Pallas kernels, attention(): pl.pallas_call(functools.partial(attend_kernel, depth), grid=(members, wi...  11.1 us
    ppermute x4, starting transfers between devices, from_behind(): return lax.ppermute(block, axis, route)  10.9 us
    pallas_call x1, Pallas kernels, gather_members(): pl.pallas_call(functools.partial(gather_kernel, groups), out_shape=jax.Sh...  10.6 us
    dot_general x6, matrix products, split_product(): jnp.einsum(equation, low, right, preferred_element_type=jnp.float32)  8.72 us
    unnamed x67, local copies, waits for them, and re-layouts  7.38 us
  transfers between devices with their start and end apart: 4, of which 2 were waited for; matrix products, arithmetic and copies ran while one was open for 9% of the time, Pallas kernels for 0%

profile of v5, /device:TPU:6, one launch (start us, length us, event | category | flops | bytes accessed | tf_op | source)
XLA Modules:
  0.0 191.5 jit_solution(9238437762670559841)
XLA Ops:
  0.7 1.6 multiply_reduce_fusion
  9.3 2.0 %multiply_convert_fusion = (bf16[256,1024]{1,0:T(8,128)(2,1)S(1)}, f32[256,1024]{1,0:T(8,128)}) fusion(f32[256,1024]{1,0:T(8,128)S(1)} %fusion.149, f32[256,1024]{1,0:T(8,128)S(1)} %fusion.57, s32[1024]{0:T(1024)S(1)} %get-tuple-element.54, s32[1024]{0:T(1024)S(1)} %get-tuple-element.55, pred[1024]{0:T(1024)(128)(4,1)S(1)} %fusion.143, ...), kind=kOutput, calls=%fused_computation.61 | convolution fusion | flops 9224192 | bytes 3695616 | tf_op jit(solution)/shard_map/jvp(rh,ch->rc)/dot_general | solution.py:195
  11.4 1.9 %collective-permute-start.1 = (bf16[2,2,128,1024]{3,2,1,0:T(8,128)(2,1)S(1)}, bf16[2,2,128,1024]{3,2,1,0:T(8,128)(2,1)}, u32[]{:S(2)}, u32[]{:S(2)}) collective-permute-start(bf16[2,2,128,1024]{3,2,1,0:T(8,128)(2,1)S(1)} %pad_maximum_fusion.own), channel_id=1, source_target_pairs={{1,0},{2,1},{3,2},{4,3},{5,4},{6,5},{7,6},{9,8},{10,9},{11,10},{12... | collective-permute-start | bytes 3145736 | tf_op jit(solution)/shard_map/ppermute | solution.py:21
  13.3 3.5 %collective-permute-start = (bf16[2,2,128,1024]{3,2,1,0:T(8,128)(2,1)S(1)}, bf16[2,2,128,1024]{3,2,1,0:T(8,128)(2,1)}, u32[]{:S(2)}, u32[]{:S(2)}) collective-permute-start(bf16[2,2,128,1024]{3,2,1,0:T(8,128)(2,1)S(1)} %pad_maximum_fusion.own), channel_id=1, source_target_pairs={{0,1},{1,2},{2,3},{3,4},{4,5},{5,6},{6,7},{8,9},{9,10},{10,11},{11... | collective-permute-start | bytes 3145736 | tf_op jit(solution)/shard_map/ppermute | solution.py:21
  17.0 2.5 %fusion.148 = f32[256,1024]{1,0:T(8,128)S(1)} fusion(bf16[256,1024]{1,0:T(8,128)(2,1)} %bitcast.89, bf16[1024,1024]{1,0:T(8,128)(2,1)} %param.20), kind=kOutput, calls=%fused_computation.223 | convolution fusion | flops 536870912 | bytes 3670016 | tf_op jit(solution)/shard_map/jvp()/dot_general | solution.py:65
  23.7 2.1 %multiply_convert_fusion.1 = (bf16[256,1024]{1,0:T(8,128)(2,1)S(1)}, f32[256,1024]{1,0:T(8,128)}) fusion(f32[256,1024]{1,0:T(8,128)S(1)} %fusion.148, f32[256,1024]{1,0:T(8,128)S(1)} %fusion.58, s32[1024]{0:T(1024)S(1)} %get-tuple-element.54, s32[1024]{0:T(1024)S(1)} %get-tuple-element.55, pred[1024]{0:T(1024)(128)(4,1)S(1)} %fusion.143, ...), kind=kOutput, calls=%fused_computation.63 | convolution fusion | flops 9224192 | bytes 3695616 | tf_op jit(solution)/shard_map/jvp(rh,ch->rc)/dot_general | solution.py:195
  25.8 13.0 %collective-permute-done.below = bf16[2,2,128,1024]{3,2,1,0:T(8,128)(2,1)} collective-permute-done((bf16[2,2,128,1024]{3,2,1,0:T(8,128)(2,1)S(1)}, bf16[2,2,128,1024]{3,2,1,0:T(8,128)(2,1)}, u32[]{:S(2)}, u32[]{:S(2)}) %collective-permute-start) | collective-permute-done | bytes 1048608 | tf_op jit(solution)/shard_map/ppermute | solution.py:21
  38.8 11.1 %shard_map.156 = bf16[2,128,1024]{2,1,0:T(8,128)(2,1)S(1)} custom-call(bf16[2,128,1024]{2,1,0:T(8,128)(2,1)S(1)} %bitcast.73, bf16[2,2,128,1024]{3,2,1,0:T(8,128)(2,1)} %collective-permute-done.below, bf16[2,2,128,1024]{3,2,1,0:T(8,128)(2,1)S(1)} %pad_maximum_fusion.own, bf16[2,2,128,1024]{3,2,1,0:T(8,128)(2,1)} %collective-permute-done.1.above), custom_call_target="tpu_custom_call" | custom-call | flops 402653184 | bytes 4194304 | tf_op jit(solution)/shard_map/pallas_call | solution.py:167
  52.5 10.6 %shard_map.157 = f32[4,2,100,128]{3,2,1,0:T(8,128)} custom-call(f32[2,100,128]{2,1,0:T(8,128)} %fusion.16.own), custom_call_target="tpu_custom_call" | custom-call | tf_op jit(solution)/shard_map/pallas_call | solution.py:226
  64.5 2.4 %multiply_reduce_fusion.1 = (f32[]{:T(128)}, f32[2,100,1024]{2,1,0:T(8,128)S(1)}) fusion(f32[100,1024]{1,0:T(8,128)} %multiply_multiply_fusion, f32[100,1024]{1,0:T(8,128)} %param.26, f32[2,100,1024]{2,1,0:T(8,128)S(1)} %fusion.53, s32[1024]{0:T(1024)S(1)} %copy-done.28, f32[2,100,128]{2,1,0:T(8,128)} %fusion.16.own), kind=kOutput, calls=%fused_computation.70 | convolution fusion | flops 54095872 | bytes 2564100 | tf_op jit(solution)/shard_map/mvt,pt->mvp/dot_general | solution.py:195
  69.5 2.0 %convolution_bitcast_fusion = bf16[1024,1024]{1,0:T(8,128)(2,1)} fusion(bf16[2,128,1024]{2,1,0:T(8,128)(2,1)S(1)} %copy-done.8, bf16[2,128,1024]{2,1,0:T(8,128)(2,1)S(1)} %convolution_convert_fusion.4), kind=kOutput, calls=%fused_computation | convolution fusion | flops 536870912 | bytes 3145728 | tf_op jit(solution)/shard_map/dot_general | solution.py:554
  72.6 16.9 %shard_map.158 = (bf16[2,128,1024]{2,1,0:T(8,128)(2,1)S(1)}, bf16[2,2,128,1024]{3,2,1,0:T(8,128)(2,1)}, f32[2,2,128,1024]{3,2,1,0:T(8,128)S(1)}, bf16[2,2,128,1024]{3,2,1,0:T(8,128)(2,1)}) custom-call(bf16[2,128,1024]{2,1,0:T(8,128)(2,1)S(1)} %bitcast.74, bf16[2,2,128,1024]{3,2,1,0:T(8,128)(2,1)} %collective-permute-done.below, ...), custom_call_target="tpu_custom_call" | custom-call | flops 1006632960 | bytes 9437184 | tf_op jit(solution)/shard_map/pallas_call | solution.py:178
  93.7 1.7 fusion.125
  97.2 1.6 copy-done.5
  98.8 45.5 %shard_map.159 = (f32[128,1024]{1,0:T(8,128)S(1)}, f32[8,16,1024]{2,1,0:T(8,128)S(1)}) custom-call(bf16[4,2,128,1024]{3,2,1,0:T(8,128)(2,1)S(1)} %bitcast.75, f32[4,2,16,1024]{3,2,1,0:T(8,128)S(1)} %bitcast.76), custom_call_target="tpu_custom_call" | custom-call | flops 40000000000 | bytes 4194304 | tf_op jit(solution)/shard_map/pallas_call | solution.py:470
  145.6 1.9 collective-permute-start.2
  147.5 3.6 %collective-permute-start.3 = (bf16[2,2,128,1024]{3,2,1,0:T(8,128)(2,1)}, bf16[2,2,128,1024]{3,2,1,0:T(8,128)(2,1)}, u32[]{:S(2)}, u32[]{:S(2)}) collective-permute-start(bf16[2,2,128,1024]{3,2,1,0:T(8,128)(2,1)} %get-tuple-element.43), channel_id=1, source_target_pairs={{0,1},{1,2},{2,3},{3,4},{4,5},{5,6},{6,7},{8,9},{9,10},{10,11},{11... | collective-permute-start | bytes 3145736 | tf_op jit(solution)/shard_map/ppermute | solution.py:21
  153.5 2.1 %fusion.55 = f32[256,1024]{1,0:T(8,128)} fusion(s32[1024]{0:T(1024)S(1)} %get-tuple-element.54, s32[1024]{0:T(1024)S(1)} %get-tuple-element.55, pred[1024]{0:T(1024)(128)(4,1)S(1)} %fusion.143, f32[256,16]{0,1:T(8,128)S(1)} %fusion.20), kind=kOutput, calls=%fused_computation.90 | convolution fusion | flops 8425472 | bytes 1074176 | tf_op jit(solution)/shard_map/transpose(jvp(rh,ch->rc))/dot_general | solution.py:65
  155.6 4.7 %fusion.10 = bf16[256,1024]{1,0:T(8,128)(2,1)} fusion(bf16[1024,1024]{1,0:T(8,128)(2,1)} %param.20, f32[256,1024]{1,0:T(8,128)} %copy-done.11, f32[256,1024]{1,0:T(8,128)} %fusion.55, f32[256,1024]{1,0:T(8,128)} %get-tuple-element.49, bf16[256,1024]{1,0:T(8,128)(2,1)S(1)} %bitcast.72, s32[1024]{0:T(1024)S(1)} %get-tuple-element.54, ...), kind=kOutput, calls=%fused_computation.21 | convolution fusion | flops 546881536 | bytes 6317056 | tf_op jit(solution)/shard_map/transpose(jvp())/dot_general | solution.py:65
  160.3 12.2 %collective-permute-done.3 = bf16[2,2,128,1024]{3,2,1,0:T(8,128)(2,1)} collective-permute-done((bf16[2,2,128,1024]{3,2,1,0:T(8,128)(2,1)}, bf16[2,2,128,1024]{3,2,1,0:T(8,128)(2,1)}, u32[]{:S(2)}, u32[]{:S(2)}) %collective-permute-start.3) | collective-permute-done | bytes 1048608 | tf_op jit(solution)/shard_map/ppermute | solution.py:21
  172.5 2.7 %add_convert_fusion = bf16[2,2,128,1024]{3,2,1,0:T(8,128)(2,1)S(1)} fusion(bf16[2,2,128,1024]{3,2,1,0:T(8,128)(2,1)} %collective-permute-done.3, f32[2,2,128,1024]{3,2,1,0:T(8,128)} %copy-done.6, bf16[2,2,128,1024]{3,2,1,0:T(8,128)(2,1)} %collective-permute-done.2), kind=kLoop, calls=%fused_computation.3 | loop fusion | flops 2621440 | bytes 5242880 | tf_op jit(solution)/shard_map/convert.4
  178.4 2.1 %fusion.56 = f32[256,1024]{1,0:T(8,128)} fusion(s32[1024]{0:T(1024)S(1)} %get-tuple-element.54, s32[1024]{0:T(1024)S(1)} %get-tuple-element.55, pred[1024]{0:T(1024)(128)(4,1)S(1)} %fusion.143, f32[256,16]{0,1:T(8,128)S(1)} %fusion.24), kind=kOutput, calls=%fused_computation.91 | convolution fusion | flops 8425472 | bytes 1074176 | tf_op jit(solution)/shard_map/transpose(jvp(rh,ch->rc))/dot_general | solution.py:68
  180.5 4.7 %convolution_convert_fusion = bf16[256,1024]{1,0:T(8,128)(2,1)} fusion(bf16[1024,1024]{1,0:T(8,128)(2,1)} %param.21, f32[256,1024]{1,0:T(8,128)} %get-tuple-element.51, bf16[256,1024]{1,0:T(8,128)(2,1)S(1)} %bitcast.86, f32[256,1024]{1,0:T(8,128)} %copy-done.9, f32[256,1024]{1,0:T(8,128)} %fusion.56, s32[1024]{0:T(1024)S(1)} %get-tuple-element.54, ...), kind=kOutput, calls=%fused_computation.20 | convolution fusion | flops 546881536 | bytes 6317056 | tf_op jit(solution)/shard_map/transpose(jvp())/dot_general | solution.py:68
  185.2 2.9 %fusion.15 = bf16[256,1024]{1,0:T(8,128)(2,1)S(1)} fusion(bf16[256,1024]{1,0:T(8,128)(2,1)} %fusion.10, bf16[256,1024]{1,0:T(8,128)(2,1)} %convolution_convert_fusion, bf16[256,1024]{1,0:T(8,128)(2,1)} %bitcast.93, bf16[1024,1024]{1,0:T(8,128)(2,1)} %param.22), kind=kOutput, calls=%fused_computation.28 | convolution fusion | flops 537657344 | bytes 4194304 | tf_op jit(solution)/shard_map/transpose(jvp())/dot_general | solution.py:71
  (105 shorter events, 31.1 us)
Async XLA Ops:
  0.6 49.3 %copy-start = (bf16[1024,1024]{1,0:T(8,128)(2,1)S(1)}, bf16[1024,1024]{1,0:T(8,128)(2,1)}, u32[]{:S(2)}) copy-start(bf16[1024,1024]{1,0:T(8,128)(2,1)} %param.23) | copy-start | bytes 6291460
  0.6 3.1 %copy-start.32 = (bf16[1024,1024]{1,0:T(8,128)(2,1)S(1)}, bf16[1024,1024]{1,0:T(8,128)(2,1)}, u32[]{:S(2)}) copy-start(bf16[1024,1024]{1,0:T(8,128)(2,1)} %param.22) | copy-start | bytes 6291460
  3.7 2.5 %copy-start.19 = (bf16[2,128,1024]{2,1,0:T(8,128)(2,1)}, bf16[2,128,1024]{2,1,0:T(8,128)(2,1)S(1)}, u32[]{:S(2)}) copy-start(bf16[2,128,1024]{2,1,0:T(8,128)(2,1)S(1)} %multiply_convert_fusion.2) | copy-start | bytes 1572868
  6.2 5.1 %copy-start.9 = (f32[256,1024]{1,0:T(8,128)}, f32[256,1024]{1,0:T(8,128)S(1)}, u32[]{:S(2)}) copy-start(f32[256,1024]{1,0:T(8,128)S(1)} %fusion.149) | copy-start | bytes 3145732
  11.4 14.4 %collective-permute-start.1 = (bf16[2,2,128,1024]{3,2,1,0:T(8,128)(2,1)S(1)}, bf16[2,2,128,1024]{3,2,1,0:T(8,128)(2,1)}, u32[]{:S(2)}, u32[]{:S(2)}) collective-permute-start(bf16[2,2,128,1024]{3,2,1,0:T(8,128)(2,1)S(1)} %pad_maximum_fusion.own), channel_id=1, source_target_pairs={{1,0},{2,1},{3,2},{4,3},{5,4},{6,5},{7,6},{9,8},{10,9},{11,10},{12... | collective-permute-start | bytes 3145736 | tf_op jit(solution)/shard_map/ppermute | solution.py:21
  13.3 25.5 %collective-permute-start = (bf16[2,2,128,1024]{3,2,1,0:T(8,128)(2,1)S(1)}, bf16[2,2,128,1024]{3,2,1,0:T(8,128)(2,1)}, u32[]{:S(2)}, u32[]{:S(2)}) collective-permute-start(bf16[2,2,128,1024]{3,2,1,0:T(8,128)(2,1)S(1)} %pad_maximum_fusion.own), channel_id=1, source_target_pairs={{0,1},{1,2},{2,3},{3,4},{4,5},{5,6},{6,7},{8,9},{9,10},{10,11},{11... | collective-permute-start | bytes 3145736 | tf_op jit(solution)/shard_map/ppermute | solution.py:21
  16.9 3.4 %copy-start.28 = (s32[1024]{0:T(1024)S(1)}, s32[1024]{0:T(1024)}, u32[]{:S(2)}) copy-start(s32[1024]{0:T(1024)} %param.29) | copy-start | bytes 12292
  17.0 3.4 %copy-start.29 = (f32[1024]{0:T(1024)S(1)}, f32[1024]{0:T(1024)}, u32[]{:S(2)}) copy-start(f32[1024]{0:T(1024)} %param.27) | copy-start | bytes 12292
  17.0 3.7 %copy-start.30 = (f32[100]{0:T(128)S(1)}, f32[100]{0:T(128)}, u32[]{:S(2)}) copy-start(f32[100]{0:T(128)} %param.28) | copy-start | bytes 1204
  19.5 6.3 %copy-start.11 = (f32[256,1024]{1,0:T(8,128)}, f32[256,1024]{1,0:T(8,128)S(1)}, u32[]{:S(2)}) copy-start(f32[256,1024]{1,0:T(8,128)S(1)} %fusion.148) | copy-start | bytes 3145732
  25.8 24.2 %copy-start.3 = (bf16[256,1024]{1,0:T(8,128)(2,1)}, bf16[256,1024]{1,0:T(8,128)(2,1)S(1)}, u32[]{:S(2)}) copy-start(bf16[256,1024]{1,0:T(8,128)(2,1)S(1)} %get-tuple-element.48) | copy-start | bytes 1572868
  38.8 11.2 %copy-start.15 = (bf16[2,128,1024]{2,1,0:T(8,128)(2,1)S(1)}, bf16[2,128,1024]{2,1,0:T(8,128)(2,1)}, u32[]{:S(2)}) copy-start(bf16[2,128,1024]{2,1,0:T(8,128)(2,1)} %param.18) | copy-start | bytes 1572868
  38.8 11.2 %copy-start.17 = (bf16[2,128,1024]{2,1,0:T(8,128)(2,1)S(1)}, bf16[2,128,1024]{2,1,0:T(8,128)(2,1)}, u32[]{:S(2)}) copy-start(bf16[2,128,1024]{2,1,0:T(8,128)(2,1)} %param.17) | copy-start | bytes 1572868
  63.2 3.8 %copy-start.25 = (f32[100,1024]{1,0:T(8,128)S(1)}, f32[100,1024]{1,0:T(8,128)}, u32[]{:S(2)}) copy-start(f32[100,1024]{1,0:T(8,128)} %multiply_multiply_fusion) | copy-start | bytes 1228804
  67.4 2.1 %copy-start.8 = (bf16[2,128,1024]{2,1,0:T(8,128)(2,1)S(1)}, bf16[2,128,1024]{2,1,0:T(8,128)(2,1)}, u32[]{:S(2)}) copy-start(bf16[2,128,1024]{2,1,0:T(8,128)(2,1)} %copy-done.7) | copy-start | bytes 1572868
  69.5 2.8 %copy-start.20 = (bf16[2,128,1024]{2,1,0:T(8,128)(2,1)}, bf16[2,128,1024]{2,1,0:T(8,128)(2,1)S(1)}, u32[]{:S(2)}) copy-start(bf16[2,128,1024]{2,1,0:T(8,128)(2,1)S(1)} %convolution_convert_fusion.4) | copy-start | bytes 1572868
  98.8 53.0 %copy-start.2 = (bf16[2,128,1024]{2,1,0:T(8,128)(2,1)S(1)}, bf16[2,128,1024]{2,1,0:T(8,128)(2,1)}, u32[]{:S(2)}) copy-start(bf16[2,128,1024]{2,1,0:T(8,128)(2,1)} %copy-done.1) | copy-start | bytes 1572868
  98.8 53.0 %copy-start.12 = (f32[256,1024]{1,0:T(8,128)S(1)}, f32[256,1024]{1,0:T(8,128)}, u32[]{:S(2)}) copy-start(f32[256,1024]{1,0:T(8,128)} %copy-done.11) | copy-start | bytes 3145732
  145.6 14.7 %collective-permute-start.2 = (bf16[2,2,128,1024]{3,2,1,0:T(8,128)(2,1)}, bf16[2,2,128,1024]{3,2,1,0:T(8,128)(2,1)}, u32[]{:S(2)}, u32[]{:S(2)}) collective-permute-start(bf16[2,2,128,1024]{3,2,1,0:T(8,128)(2,1)} %get-tuple-element.42), channel_id=1, source_target_pairs={{1,0},{2,1},{3,2},{4,3},{5,4},{6,5},{7,6},{9,8},{10,9},{11,10},{12... | collective-permute-start | bytes 3145736 | tf_op jit(solution)/shard_map/ppermute | solution.py:21
  147.5 25.0 %collective-permute-start.3 = (bf16[2,2,128,1024]{3,2,1,0:T(8,128)(2,1)}, bf16[2,2,128,1024]{3,2,1,0:T(8,128)(2,1)}, u32[]{:S(2)}, u32[]{:S(2)}) collective-permute-start(bf16[2,2,128,1024]{3,2,1,0:T(8,128)(2,1)} %get-tuple-element.43), channel_id=1, source_target_pairs={{0,1},{1,2},{2,3},{3,4},{4,5},{5,6},{6,7},{8,9},{9,10},{10,11},{11... | collective-permute-start | bytes 3145736 | tf_op jit(solution)/shard_map/ppermute | solution.py:21
  185.2 2.9 %copy-start.16 = (bf16[2,128,1024]{2,1,0:T(8,128)(2,1)S(1)}, bf16[2,128,1024]{2,1,0:T(8,128)(2,1)}, u32[]{:S(2)}) copy-start(bf16[2,128,1024]{2,1,0:T(8,128)(2,1)} %param.18) | copy-start | bytes 1572868
  185.2 2.9 %copy-start.18 = (bf16[2,128,1024]{2,1,0:T(8,128)(2,1)S(1)}, bf16[2,128,1024]{2,1,0:T(8,128)(2,1)}, u32[]{:S(2)}) copy-start(bf16[2,128,1024]{2,1,0:T(8,128)(2,1)} %param.17) | copy-start | bytes 1572868
  185.2 2.9 %copy-start.27 = (f32[1024]{0:T(1024)S(1)}, f32[1024]{0:T(1024)}, u32[]{:S(2)}) copy-start(f32[1024]{0:T(1024)} %param.19) | copy-start | bytes 12292
  185.2 3.2 %copy-start.21 = (bf16[2,128,1024]{2,1,0:T(8,128)(2,1)S(1)}, bf16[2,128,1024]{2,1,0:T(8,128)(2,1)}, u32[]{:S(2)}) copy-start(bf16[2,128,1024]{2,1,0:T(8,128)(2,1)} %copy-done.20) | copy-start | bytes 1572868
  (13 other events, 16.0 us)
